TPU v7x, 128 devices: a whole 4x4x4 slice. The times are simulated.
128 devices in a mesh: gx: 8 (over y_hi, x), gy: 16 (over y_lo, z, core).
Axes of the slice: x: 4, y: 4 (y_hi: 2, y_lo: 2; y = y_hi * 2 + y_lo), z: 4, core: 2. Of those that a mesh axis runs over, the one named last changes fastest.
Arguments:
- features: bfloat16 [32, 64, 128, 128], P(None, 'gx', 'gy'), may hold values from -6 to 6
- weight_two: bfloat16 [27, 32, 32], replicated, may hold values from -0.21875 to 0.21875
- bias_two: float32 [32], replicated, may hold values from -3 to 3
- weight_three: bfloat16 [27, 64, 32], replicated, may hold values from -0.21875 to 0.21875
- bias_three: float32 [64], replicated, may hold values from -3 to 3
- weight_four: bfloat16 [27, 128, 64], replicated, may hold values from -0.25 to 0.25
- bias_four: float32 [128], replicated, may hold values from -3 to 3
Outputs:
- level_two: bfloat16 [32, 64, 128, 128], P(None, 'gx', 'gy')
- level_three: bfloat16 [64, 32, 64, 64], P(None, 'gx', 'gy')
- bottleneck: bfloat16 [128, 16, 32, 32], P(None, None, None, 'gy')
All inputs are finite; a program needn't handle non-finite values.
Results may differ from a plain program's by a relative error of at most 0.0085.
Values may be sent and summed in bfloat16 or wider, within the bound.
A program may use at most 64 MiB of HBM per device.

v0:
```python
import jax
import jax.numpy as jnp
from jax import lax
from jax.sharding import PartitionSpec as P


def extended(cells, sides, width):
    for axis, dim in sides:
        count = lax.axis_size(axis)
        head = lax.slice_in_dim(cells, 0, width, axis=dim)
        tail = lax.slice_in_dim(cells, cells.shape[dim] - width, cells.shape[dim], axis=dim)
        cells = jnp.concatenate(
            [
                lax.ppermute(tail, axis, [(i, (i + 1) % count) for i in range(count)]),
                cells,
                lax.ppermute(head, axis, [((i + 1) % count, i) for i in range(count)]),
            ],
            axis=dim,
        )
    return cells


def laid_out(blocks, dim):
    blocks = jnp.moveaxis(blocks, 0, dim)
    shape = blocks.shape
    return blocks.reshape(*shape[:dim], shape[dim] * shape[dim + 1], *shape[dim + 2 :])


def sent_to_all(array, axis):
    copies = jnp.broadcast_to(array, (lax.axis_size(axis), *array.shape))
    return lax.all_to_all(copies, axis, split_axis=0, concat_axis=0, tiled=True)


def gathered_copies(array, axis, dim):
    return laid_out(sent_to_all(array, axis), dim)


def wrap_axis(source, axis):
    first = lax.slice_in_dim(source, 0, 1, axis=axis)
    final = lax.slice_in_dim(source, source.shape[axis] - 1, source.shape[axis], axis=axis)
    return jnp.concatenate([final, source, first], axis=axis)


def convolve(padded, weights, bias_values):
    in_channels = padded.shape[0]
    extent_x = padded.shape[1] - 2
    extent_y = padded.shape[2] - 2
    extent_z = padded.shape[3] - 2
    out_channels = weights.shape[1]
    running = jnp.zeros((out_channels, extent_x * extent_y * extent_z), jnp.float32)
    for offset_x in range(3):
        for offset_y in range(3):
            stacked = jnp.concatenate(
                [
                    padded[
                        :,
                        offset_x : offset_x + extent_x,
                        offset_y : offset_y + extent_y,
                        offset_z : offset_z + extent_z,
                    ]
                    for offset_z in range(3)
                ],
                axis=0,
            ).reshape(3 * in_channels, -1)
            first_row = offset_x * 9 + offset_y * 3
            mixing = (
                weights[first_row : first_row + 3]
                .transpose(1, 0, 2)
                .reshape(out_channels, 3 * in_channels)
            )
            running = running + jnp.dot(mixing, stacked, preferred_element_type=jnp.float32)
    result = running + bias_values[:, None]
    result = jax.nn.leaky_relu(result, 0.1).astype(jnp.bfloat16)
    return result.reshape(out_channels, extent_x, extent_y, extent_z)


def average_pool(source):
    channels, extent_x, extent_y, extent_z = source.shape
    blocks = source.astype(jnp.float32).reshape(
        channels, extent_x // 2, 2, extent_y // 2, 2, extent_z // 2, 2
    )
    return blocks.mean(axis=(2, 4, 6)).astype(jnp.bfloat16)


def shards(features, weight_two, bias_two, weight_three, bias_three, weight_four, bias_four):
    rimmed = extended(features, (("gx", 1), ("gy", 2)), 1)
    level_two = convolve(wrap_axis(rimmed, 3), weight_two, bias_two)
    pooled = average_pool(level_two)
    rimmed_three = extended(pooled, (("gx", 1), ("gy", 2)), 1)
    level_three = convolve(wrap_axis(rimmed_three, 3), weight_three, bias_three)
    coarse = average_pool(level_three)
    rimmed_four = extended(coarse, (("gx", 1), ("gy", 2)), 1)
    columns = convolve(wrap_axis(rimmed_four, 3), weight_four, bias_four)
    gathered_out = gathered_copies(columns, "gx", 1)
    bottleneck = lax.all_to_all(gathered_out, "gy", split_axis=3, concat_axis=2, tiled=True)
    return (level_two, level_three, bottleneck)


def solution(mesh):
    return jax.shard_map(
        shards,
        mesh=mesh,
        in_specs=(P(None, "gx", "gy", None), P(), P(), P(), P(), P(), P()),
        out_specs=(P(None, "gx", "gy", None), P(None, "gx", "gy", None), P(None, None, None, "gy")),
        check_vma=False,
    )
```

profile of v0, /device:TPU:1, one launch (start us, length us, event | category | flops | bytes accessed | tf_op | source)
XLA Modules:
  0.0 117.7 jit_solution(15931731363312359776)
XLA Ops:
  0.6 1.5 %copy.158 = bf16[32,8,8,128]{3,0,2,1:T(8,128)(2,1)S(1)} copy(bf16[32,8,8,128]{3,2,1,0:T(8,128)(2,1)} %param.7) | data formatting | bytes 1048576 | tf_op args[0]
  2.1 2.1 %collective-permute-start = (bf16[32,1,8,128]{3,0,2,1:T(8,128)(2,1)S(1)}, bf16[32,1,8,128]{3,0,2,1:T(8,128)(2,1)S(1)}, u32[]{:S(2)}, u32[]{:S(2)}) collective-permute-start(bf16[32,1,8,128]{3,0,2,1:T(8,128)(2,1)S(1)} %get-tuple-element.72), channel_id=1, source_target_pairs={{0,16},{16,32},{32,48},{48,64},{64,80},{80,96},{96,112},{112,0},{1... | collective-permute-start | bytes 196616 | tf_op jit(solution)/shard_map/ppermute | solution.py:14
  4.2 4.0 %collective-permute-start.1 = (bf16[32,1,8,128]{3,0,2,1:T(8,128)(2,1)S(1)}, bf16[32,1,8,128]{3,0,2,1:T(8,128)(2,1)S(1)}, u32[]{:S(2)}, u32[]{:S(2)}) collective-permute-start(bf16[32,1,8,128]{3,0,2,1:T(8,128)(2,1)S(1)} %get-tuple-element.71), channel_id=1, source_target_pairs={{16,0},{32,16},{48,32},{64,48},{80,64},{96,80},{112,96},{0,112},{1... | collective-permute-start | bytes 196616 | tf_op jit(solution)/shard_map/ppermute | solution.py:16
  8.2 1.6 %collective-permute-done = bf16[32,1,8,128]{3,0,2,1:T(8,128)(2,1)S(1)} collective-permute-done((bf16[32,1,8,128]{3,0,2,1:T(8,128)(2,1)S(1)}, bf16[32,1,8,128]{3,0,2,1:T(8,128)(2,1)S(1)}, u32[]{:S(2)}, u32[]{:S(2)}) %collective-permute-start) | collective-permute-done | bytes 65568 | tf_op jit(solution)/shard_map/ppermute | solution.py:14
  10.2 1.8 %collective-permute-start.3 = (bf16[32,10,1,128]{3,0,2,1:T(8,128)(2,1)S(1)}, bf16[32,10,1,128]{3,0,2,1:T(8,128)(2,1)S(1)}, u32[]{:S(2)}, u32[]{:S(2)}) collective-permute-start(bf16[32,10,1,128]{3,0,2,1:T(8,128)(2,1)S(1)} %get-tuple-element.67), channel_id=1, source_target_pairs={{1,0},{2,1},{3,2},{4,3},{5,4},{6,5},{7,6},{8,7},{9,8},{10,9},{11,1... | collective-permute-start | bytes 245768 | tf_op jit(solution)/shard_map/ppermute | solution.py:16
  12.0 1.7 %collective-permute-start.2 = (bf16[32,10,1,128]{3,0,2,1:T(8,128)(2,1)S(1)}, bf16[32,10,1,128]{3,0,2,1:T(8,128)(2,1)S(1)}, u32[]{:S(2)}, u32[]{:S(2)}) collective-permute-start(bf16[32,10,1,128]{3,0,2,1:T(8,128)(2,1)S(1)} %get-tuple-element.66), channel_id=1, source_target_pairs={{0,1},{1,2},{2,3},{3,4},{4,5},{5,6},{6,7},{7,8},{8,9},{9,10},{10,1... | collective-permute-start | bytes 245768 | tf_op jit(solution)/shard_map/ppermute | solution.py:14
  14.7 1.0 collective-permute-done.3
  16.6 1.7 %maximum_maximum_fusion = (bf16[32,10,10,129]{3,0,2,1:T(8,128)(2,1)S(1)}, bf16[32,10,10,129]{3,0,2,1:T(8,128)(2,1)S(1)}) fusion(bf16[32,10,1,128]{3,0,2,1:T(8,128)(2,1)S(1)} %collective-permute-done.3, bf16[32,10,8,128]{3,0,2,1:T(8,128)(2,1)S(1)} %constant_dynamic-update-slice_fusion, bf16[32,10,1,128]{3,0,2,1:T(8,128)(2,1)S(1)} %collective-permute-done.2, ...), kind=kLoop, calls=%fused_computation.11 | loop fusion | flops 6604800 | bytes 2483200 | tf_op jit(solution)/shard_map/concatenate | solution.py:41
  18.3 2.8 %fusion.56 = (bf16[32,8,8,128]{3,0,2,1:T(8,128)(2,1)S(1)}, bf16[32,8,8,128]{3,0,2,1:T(8,128)(2,1)S(1)}, bf16[32,8,8,128]{3,0,2,1:T(8,128)(2,1)S(1)}, bf16[32,8,8...) fusion(bf16[32,10,10,129]{3,0,2,1:T(8,128)(2,1)S(1)} %get-tuple, ...), kind=kLoop, calls=%fused_computation.155 | loop fusion | bytes 18874368 | tf_op jit(solution)/shard_map/slice | solution.py:55
  21.5 0.6 copy.161
  22.6 0.6 copy.164
  23.4 0.6 copy.166
  24.1 0.6 copy.168
  24.7 0.6 copy.171
  25.5 0.6 copy.173
  26.6 0.6 copy.175
  27.2 0.6 copy.178
  27.8 0.6 copy.180
  28.4 1.1 fusion.18
  29.5 1.1 convolution_add_fusion.7
  30.7 1.1 convolution_add_fusion.6
  31.8 1.1 convolution_add_fusion.5
  32.9 1.1 convolution_add_fusion.4
  34.0 1.1 convolution_add_fusion.3
  35.1 1.1 convolution_add_fusion.2
  36.3 1.1 convolution_add_fusion.1
  37.4 1.1 fusion.31
  38.6 2.4 %copy.182 = f32[32,8192]{0,1:T(8,128)} copy(bf16[32,8192]{1,0:T(8,128)(2,1)S(1)} %fusion.31) | data formatting | bytes 1572864 | tf_op jit(solution)/shard_map/convert_element_type | solution.py:79
  40.9 4.8 %reduce_sum.18 = f32[32,4,4,64]{0,3,2,1:T(8,128)S(1)} reduce(f32[32,4,2,4,2,64,2]{0,6,5,4,3,2,1:T(2,128)} %bitcast.215, f32[]{:T(128)} %constant.6.clone.1), dimensions={2,4,6}, to_apply=%region_0.1 | reduce | flops 229376 | bytes 1179652 | tf_op jit(solution)/shard_map/reduce_sum | solution.py:82
  45.9 5.3 %collective-permute-start.5 = (bf16[32,1,4,64]{0,3,2,1:T(8,128)(2,1)S(1)}, bf16[32,1,4,64]{0,3,2,1:T(8,128)(2,1)S(1)}, u32[]{:S(2)}, u32[]{:S(2)}) collective-permute-start(bf16[32,1,4,64]{0,3,2,1:T(8,128)(2,1)S(1)} %get-tuple-element.96), channel_id=1, source_target_pairs={{16,0},{32,16},{48,32},{64,48},{80,64},{96,80},{112,96},{0,112},{1... | collective-permute-start | bytes 49160 | tf_op jit(solution)/shard_map/ppermute | solution.py:16
  51.2 1.3 %collective-permute-done.5 = bf16[32,1,4,64]{0,3,2,1:T(8,128)(2,1)S(1)} collective-permute-done((bf16[32,1,4,64]{0,3,2,1:T(8,128)(2,1)S(1)}, bf16[32,1,4,64]{0,3,2,1:T(8,128)(2,1)S(1)}, u32[]{:S(2)}, u32[]{:S(2)}) %collective-permute-start.5) | collective-permute-done | bytes 16416 | tf_op jit(solution)/shard_map/ppermute | solution.py:16
  52.6 5.4 %collective-permute-done.4 = bf16[32,1,4,64]{0,3,2,1:T(8,128)(2,1)S(1)} collective-permute-done((bf16[32,1,4,64]{0,3,2,1:T(8,128)(2,1)S(1)}, bf16[32,1,4,64]{0,3,2,1:T(8,128)(2,1)S(1)}, u32[]{:S(2)}, u32[]{:S(2)}) %collective-permute-start.4) | collective-permute-done | bytes 16416 | tf_op jit(solution)/shard_map/ppermute | solution.py:14
  58.0 6.7 %collective-permute-start.7 = (bf16[32,6,1,64]{0,3,2,1:T(8,128)(2,1)S(1)}, bf16[32,6,1,64]{0,3,2,1:T(8,128)(2,1)S(1)}, u32[]{:S(2)}, u32[]{:S(2)}) collective-permute-start(bf16[32,6,1,64]{0,3,2,1:T(8,128)(2,1)S(1)} %get-tuple-element.91), channel_id=1, source_target_pairs={{1,0},{2,1},{3,2},{4,3},{5,4},{6,5},{7,6},{8,7},{9,8},{10,9},{11,1... | collective-permute-start | bytes 73736 | tf_op jit(solution)/shard_map/ppermute | solution.py:16
  64.7 0.9 collective-permute-done.7
  65.7 0.7 collective-permute-done.6
  69.0 0.7 fusion.46
  73.5 1.5 %collective-permute-start.8 = (bf16[64,1,2,32]{0,3,2,1:T(8,128)(2,1)S(1)}, bf16[64,1,2,32]{0,3,2,1:T(8,128)(2,1)S(1)}, u32[]{:S(2)}, u32[]{:S(2)}) collective-permute-start(bf16[64,1,2,32]{0,3,2,1:T(8,128)(2,1)S(1)} %get-tuple-element.146), channel_id=1, source_target_pairs={{0,16},{16,32},{32,48},{48,64},{64,80},{80,96},{96,112},{112,0},{1... | collective-permute-start | bytes 24584 | tf_op jit(solution)/shard_map/ppermute | solution.py:14
  75.0 1.1 collective-permute-done.9
  76.1 3.7 %collective-permute-done.8 = bf16[64,1,2,32]{0,3,2,1:T(8,128)(2,1)S(1)} collective-permute-done((bf16[64,1,2,32]{0,3,2,1:T(8,128)(2,1)S(1)}, bf16[64,1,2,32]{0,3,2,1:T(8,128)(2,1)S(1)}, u32[]{:S(2)}, u32[]{:S(2)}) %collective-permute-start.8) | collective-permute-done | bytes 8224 | tf_op jit(solution)/shard_map/ppermute | solution.py:14
  79.8 5.8 %collective-permute-start.11 = (bf16[64,4,1,32]{0,3,2,1:T(8,128)(2,1)S(1)}, bf16[64,4,1,32]{0,3,2,1:T(8,128)(2,1)S(1)}, u32[]{:S(2)}, u32[]{:S(2)}) collective-permute-start(bf16[64,4,1,32]{0,3,2,1:T(8,128)(2,1)S(1)} %get-tuple-element.142), channel_id=1, source_target_pairs={{1,0},{2,1},{3,2},{4,3},{5,4},{6,5},{7,6},{8,7},{9,8},{10,9},{11,1... | collective-permute-start | bytes 49160 | tf_op jit(solution)/shard_map/ppermute | solution.py:16
  85.7 0.8 collective-permute-done.11
  89.4 10.1 %all_to_all.23 = bf16[8,128,2,2,32]{1,4,3,2,0:T(8,128)(2,1)S(1)} all-to-all(bf16[8,128,2,2,32]{1,4,3,2,0:T(8,128)(2,1)S(1)} %broadcast_in_dim.2), channel_id=1, replica_groups=mesh['gx'=8,'gy'=16] {'gx'}, dimensions={0} | all-to-all | bytes 524288 | tf_op jit(solution)/shard_map/all_to_all | solution.py:31
  99.5 0.9 copy.184
  100.4 9.1 %all-to-all-start.1 = ((bf16[128,16,2,32]{0,2,1,3:T(2,128)(2,1)}), bf16[128,16,2,32]{0,2,1,3:T(2,128)(2,1)S(1)}, u32[]{:S(2)}, u32[]{:S(2)}) async-start(bf16[128,16,2,32]{0,2,1,3:T(2,128)(2,1)} %copy.184), calls=%async_computation.1 | async-start | bytes 524288 | tf_op jit(solution)/shard_map/all_to_all | solution.py:95
  109.5 0.9 copy.197
  110.4 0.9 reshape.228
  111.3 5.4 %all-to-all-done.1 = bf16[128,16,2,32]{0,2,1,3:T(2,128)(2,1)S(1)} async-done(((bf16[128,16,2,32]{0,2,1,3:T(2,128)(2,1)}), bf16[128,16,2,32]{0,2,1,3:T(2,128)(2,1)S(1)}, u32[]{:S(2)}, u32[]{:S(2)}) %all-to-all-start.1) | async-done | bytes 262176 | tf_op jit(solution)/shard_map/all_to_all | solution.py:95
  116.8 0.9 copy.187
  (113 shorter events, 13.2 us)
Async XLA Ops:
  0.6 9.2 %copy-start = (bf16[32,8,8,128]{3,2,1,0:T(8,128)(2,1)S(1)}, bf16[32,8,8,128]{3,2,1,0:T(8,128)(2,1)}, u32[]{:S(2)}) copy-start(bf16[32,8,8,128]{3,2,1,0:T(8,128)(2,1)} %param.7) | copy-start | bytes 1572868
  0.6 13.1 %copy-start.2 = (bf16[27,32,32]{2,1,0:T(8,128)(2,1)S(1)}, bf16[27,32,32]{2,1,0:T(8,128)(2,1)}, u32[]{:S(2)}) copy-start(bf16[27,32,32]{2,1,0:T(8,128)(2,1)} %param.8) | copy-start | bytes 165892
  2.1 7.7 %collective-permute-start = (bf16[32,1,8,128]{3,0,2,1:T(8,128)(2,1)S(1)}, bf16[32,1,8,128]{3,0,2,1:T(8,128)(2,1)S(1)}, u32[]{:S(2)}, u32[]{:S(2)}) collective-permute-start(bf16[32,1,8,128]{3,0,2,1:T(8,128)(2,1)S(1)} %get-tuple-element.72), channel_id=1, source_target_pairs={{0,16},{16,32},{32,48},{48,64},{64,80},{80,96},{96,112},{112,0},{1... | collective-permute-start | bytes 196616 | tf_op jit(solution)/shard_map/ppermute | solution.py:14
  4.2 5.9 %collective-permute-start.1 = (bf16[32,1,8,128]{3,0,2,1:T(8,128)(2,1)S(1)}, bf16[32,1,8,128]{3,0,2,1:T(8,128)(2,1)S(1)}, u32[]{:S(2)}, u32[]{:S(2)}) collective-permute-start(bf16[32,1,8,128]{3,0,2,1:T(8,128)(2,1)S(1)} %get-tuple-element.71), channel_id=1, source_target_pairs={{16,0},{32,16},{48,32},{64,48},{80,64},{96,80},{112,96},{0,112},{1... | collective-permute-start | bytes 196616 | tf_op jit(solution)/shard_map/ppermute | solution.py:16
  10.2 5.5 %collective-permute-start.3 = (bf16[32,10,1,128]{3,0,2,1:T(8,128)(2,1)S(1)}, bf16[32,10,1,128]{3,0,2,1:T(8,128)(2,1)S(1)}, u32[]{:S(2)}, u32[]{:S(2)}) collective-permute-start(bf16[32,10,1,128]{3,0,2,1:T(8,128)(2,1)S(1)} %get-tuple-element.67), channel_id=1, source_target_pairs={{1,0},{2,1},{3,2},{4,3},{5,4},{6,5},{7,6},{8,7},{9,8},{10,9},{11,1... | collective-permute-start | bytes 245768 | tf_op jit(solution)/shard_map/ppermute | solution.py:16
  12.0 4.2 %collective-permute-start.2 = (bf16[32,10,1,128]{3,0,2,1:T(8,128)(2,1)S(1)}, bf16[32,10,1,128]{3,0,2,1:T(8,128)(2,1)S(1)}, u32[]{:S(2)}, u32[]{:S(2)}) collective-permute-start(bf16[32,10,1,128]{3,0,2,1:T(8,128)(2,1)S(1)} %get-tuple-element.66), channel_id=1, source_target_pairs={{0,1},{1,2},{2,3},{3,4},{4,5},{5,6},{6,7},{7,8},{8,9},{9,10},{10,1... | collective-permute-start | bytes 245768 | tf_op jit(solution)/shard_map/ppermute | solution.py:14
  36.3 1.1 copy-start.6
  45.8 18.9 %copy-start.3 = (bf16[27,64,32]{1,2,0:T(8,128)(2,1)S(1)}, bf16[27,64,32]{1,2,0:T(8,128)(2,1)}, u32[]{:S(2)}) copy-start(bf16[27,64,32]{1,2,0:T(8,128)(2,1)} %param.10) | copy-start | bytes 331780
  45.9 6.7 %collective-permute-start.5 = (bf16[32,1,4,64]{0,3,2,1:T(8,128)(2,1)S(1)}, bf16[32,1,4,64]{0,3,2,1:T(8,128)(2,1)S(1)}, u32[]{:S(2)}, u32[]{:S(2)}) collective-permute-start(bf16[32,1,4,64]{0,3,2,1:T(8,128)(2,1)S(1)} %get-tuple-element.96), channel_id=1, source_target_pairs={{16,0},{32,16},{48,32},{64,48},{80,64},{96,80},{112,96},{0,112},{1... | collective-permute-start | bytes 49160 | tf_op jit(solution)/shard_map/ppermute | solution.py:16
  51.2 6.7 %collective-permute-start.4 = (bf16[32,1,4,64]{0,3,2,1:T(8,128)(2,1)S(1)}, bf16[32,1,4,64]{0,3,2,1:T(8,128)(2,1)S(1)}, u32[]{:S(2)}, u32[]{:S(2)}) collective-permute-start(bf16[32,1,4,64]{0,3,2,1:T(8,128)(2,1)S(1)} %get-tuple-element.95), channel_id=1, source_target_pairs={{0,16},{16,32},{32,48},{48,64},{64,80},{80,96},{96,112},{112,0},{1... | collective-permute-start | bytes 49160 | tf_op jit(solution)/shard_map/ppermute | solution.py:14
  58.0 7.7 %collective-permute-start.7 = (bf16[32,6,1,64]{0,3,2,1:T(8,128)(2,1)S(1)}, bf16[32,6,1,64]{0,3,2,1:T(8,128)(2,1)S(1)}, u32[]{:S(2)}, u32[]{:S(2)}) collective-permute-start(bf16[32,6,1,64]{0,3,2,1:T(8,128)(2,1)S(1)} %get-tuple-element.91), channel_id=1, source_target_pairs={{1,0},{2,1},{3,2},{4,3},{5,4},{6,5},{7,6},{8,7},{9,8},{10,9},{11,1... | collective-permute-start | bytes 73736 | tf_op jit(solution)/shard_map/ppermute | solution.py:16
  64.7 1.6 %collective-permute-start.6 = (bf16[32,6,1,64]{0,3,2,1:T(8,128)(2,1)S(1)}, bf16[32,6,1,64]{0,3,2,1:T(8,128)(2,1)S(1)}, u32[]{:S(2)}, u32[]{:S(2)}) collective-permute-start(bf16[32,6,1,64]{0,3,2,1:T(8,128)(2,1)S(1)} %get-tuple-element.90), channel_id=1, source_target_pairs={{0,1},{1,2},{2,3},{3,4},{4,5},{5,6},{6,7},{7,8},{8,9},{9,10},{10,1... | collective-permute-start | bytes 73736 | tf_op jit(solution)/shard_map/ppermute | solution.py:14
  71.9 0.8 copy-start.4
  72.4 13.2 %copy-start.1 = (bf16[27,128,64]{1,2,0:T(8,128)(2,1)S(1)}, bf16[27,128,64]{1,2,0:T(8,128)(2,1)}, u32[]{:S(2)}) copy-start(bf16[27,128,64]{1,2,0:T(8,128)(2,1)} %param.12) | copy-start | bytes 1327108
  73.4 2.7 %collective-permute-start.9 = (bf16[64,1,2,32]{0,3,2,1:T(8,128)(2,1)S(1)}, bf16[64,1,2,32]{0,3,2,1:T(8,128)(2,1)S(1)}, u32[]{:S(2)}, u32[]{:S(2)}) collective-permute-start(bf16[64,1,2,32]{0,3,2,1:T(8,128)(2,1)S(1)} %get-tuple-element.147), channel_id=1, source_target_pairs={{16,0},{32,16},{48,32},{64,48},{80,64},{96,80},{112,96},{0,112},{1... | collective-permute-start | bytes 24584 | tf_op jit(solution)/shard_map/ppermute | solution.py:16
  73.5 6.3 %collective-permute-start.8 = (bf16[64,1,2,32]{0,3,2,1:T(8,128)(2,1)S(1)}, bf16[64,1,2,32]{0,3,2,1:T(8,128)(2,1)S(1)}, u32[]{:S(2)}, u32[]{:S(2)}) collective-permute-start(bf16[64,1,2,32]{0,3,2,1:T(8,128)(2,1)S(1)} %get-tuple-element.146), channel_id=1, source_target_pairs={{0,16},{16,32},{32,48},{48,64},{64,80},{80,96},{96,112},{112,0},{1... | collective-permute-start | bytes 24584 | tf_op jit(solution)/shard_map/ppermute | solution.py:14
  79.8 6.7 %collective-permute-start.11 = (bf16[64,4,1,32]{0,3,2,1:T(8,128)(2,1)S(1)}, bf16[64,4,1,32]{0,3,2,1:T(8,128)(2,1)S(1)}, u32[]{:S(2)}, u32[]{:S(2)}) collective-permute-start(bf16[64,4,1,32]{0,3,2,1:T(8,128)(2,1)S(1)} %get-tuple-element.142), channel_id=1, source_target_pairs={{1,0},{2,1},{3,2},{4,3},{5,4},{6,5},{7,6},{8,7},{9,8},{10,9},{11,1... | collective-permute-start | bytes 49160 | tf_op jit(solution)/shard_map/ppermute | solution.py:16
  85.6 1.2 %collective-permute-start.10 = (bf16[64,4,1,32]{0,3,2,1:T(8,128)(2,1)S(1)}, bf16[64,4,1,32]{0,3,2,1:T(8,128)(2,1)S(1)}, u32[]{:S(2)}, u32[]{:S(2)}) collective-permute-start(bf16[64,4,1,32]{0,3,2,1:T(8,128)(2,1)S(1)} %get-tuple-element.141), channel_id=1, source_target_pairs={{0,1},{1,2},{2,3},{3,4},{4,5},{5,6},{6,7},{7,8},{8,9},{9,10},{10,1... | collective-permute-start | bytes 49160 | tf_op jit(solution)/shard_map/ppermute | solution.py:14
  87.4 1.8 %copy-start.5 = (f32[128]{0:T(128)S(1)}, f32[128]{0:T(128)}, u32[]{:S(2)}) copy-start(f32[128]{0:T(128)} %param.13) | copy-start | bytes 1540
  100.4 16.3 %all-to-all-start.1 = ((bf16[128,16,2,32]{0,2,1,3:T(2,128)(2,1)}), bf16[128,16,2,32]{0,2,1,3:T(2,128)(2,1)S(1)}, u32[]{:S(2)}, u32[]{:S(2)}) async-start(bf16[128,16,2,32]{0,2,1,3:T(2,128)(2,1)} %copy.184), calls=%async_computation.1 | async-start | bytes 524288 | tf_op jit(solution)/shard_map/all_to_all | solution.py:95
where the time goes:
time: 118 us
  starting transfers between devices  38 us (32%)
  waiting for transfers between devices  22.8 us (19%)
  local copies, waits for them, and re-layouts  19.6 us (17%)
  matrix products  13.5 us (11%)
  other arithmetic  12.2 us (10%)
  blocking collectives  10.1 us (9%)
  between operations  1.41 us (1%)
    ppermute x6, starting transfers between devices, extended(): lax.ppermute(head, axis, [((i + 1) % count, i) for i in range(count)])  23.7 us
    dot_general x27, matrix products, convolve(): jnp.dot(mixing, stacked, preferred_element_type=jnp.float32)  13.5 us
    ppermute x6, waiting for transfers between devices, extended(): lax.ppermute(tail, axis, [(i, (i + 1) % count) for i in range(count)])  12.2 us
    all_to_all x1, blocking collectives, sent_to_all(): return lax.all_to_all(copies, axis, split_axis=0, concat_axis=0, tiled=True)  10.1 us
    all_to_all x1, starting transfers between devices, shards(): lax.all_to_all(gathered_out, 'gy', split_axis=3, concat_axis=2, tiled=True)  9.07 us
    concatenate x9, local copies, waits for them, and re-layouts, convolve(): jnp.concatenate([padded[:, offset_x:offset_x + extent_x, offset_y:offset_...  5.49 us
    all_to_all x1, waiting for transfers between devices, shards(): lax.all_to_all(gathered_out, 'gy', split_axis=3, concat_axis=2, tiled=True)  5.44 us
    ppermute x6, starting transfers between devices, extended(): lax.ppermute(tail, axis, [(i, (i + 1) % count) for i in range(count)])  5.26 us
  transfers between devices with their start and end apart: 13, of which 12 were waited for; matrix products, arithmetic and copies ran while one was open for 3% of the time, Pallas kernels for 0%

commit v1 on v0

v1 whole, which is shorter than its diff:
```python
import functools

import jax
import jax.numpy as jnp
import numpy as np
from jax import lax
from jax.experimental import pallas as pl
from jax.experimental.pallas import tpu as pltpu
from jax.sharding import PartitionSpec as P

BF = jnp.bfloat16
F32 = jnp.float32
MESH = pl.DeviceIdType.MESH


def tables():
    parts, at, row = [], {}, 0

    def add(name, matrix):
        nonlocal row
        rows, lanes = matrix.shape
        full = np.zeros((-(-rows // 16) * 16, 256), np.float32)
        full[:rows, :lanes] = matrix
        at[name] = row
        parts.append(full)
        row += full.shape[0]

    select = np.zeros((64, 256))
    for c in range(32):
        select[c, c * 8] = 1
        select[32 + c, c * 8 + 7] = 1
    add("select_two", select)
    spread = np.zeros((8, 128, 256))
    for y in range(8):
        for dy in range(3):
            if 0 <= y + dy - 1 < 8:
                for c in range(32):
                    spread[y, dy * 32 + c, c * 8 + y + dy - 1] = 1
    add("spread_two", spread.reshape(1024, 256))
    order = np.zeros((256, 256))
    for y in range(8):
        for o in range(32):
            order[o * 8 + y, y * 32 + o] = 1
    add("order_two", order)
    edge = np.zeros((256, 64))
    for o in range(32):
        edge[o * 8, o] = 1
        edge[o * 8 + 7, 32 + o] = 1
    add("edge_two", edge)
    pool = np.zeros((2, 2, 128, 128))
    for half in range(2):
        for x in range(2):
            for z in range(128):
                pool[half, x, z, half * 64 + z // 2] = 0.125
    add("pool_two", pool.reshape(512, 128))
    select = np.zeros((64, 128))
    for c in range(32):
        select[c, c * 4] = 1
        select[32 + c, c * 4 + 3] = 1
    add("select_three", select)
    add("unit", np.eye(64))
    spread = np.zeros((4, 128, 128))
    for y in range(4):
        for dy in range(3):
            if 0 <= y + dy - 1 < 4:
                for c in range(32):
                    spread[y, dy * 32 + c, c * 4 + y + dy - 1] = 1
    add("spread_three", spread.reshape(512, 128))
    order = np.zeros((256, 256))
    for y in range(4):
        for o in range(64):
            order[o * 4 + y, y * 64 + o] = 1
    add("order_three", order)
    edge = np.zeros((256, 128))
    for o in range(64):
        edge[o * 4, o] = 1
        edge[o * 4 + 3, 64 + o] = 1
    add("edge_three", edge)
    pick = np.zeros((2, 16, 2, 2, 2, 4, 64))
    for odd in range(2):
        for target in range(16):
            for half in range(2):
                z = (2 * target - 1 + 2 * half + odd) % 32
                for x in range(2):
                    pick[odd, target, half, x, :, 2 * x : 2 * x + 2, 2 * z : 2 * z + 2] = 0.125
    add("pick_four", pick.reshape(256, 256))
    gather = np.zeros((2, 256, 128))
    for odd in range(2):
        for o in range(64):
            gather[odd, o * 4 : o * 4 + 4, odd * 64 + o] = 1
    add("gather_four", gather.reshape(512, 128))
    turn = np.zeros((3, 2, 2, 32, 16, 2, 2, 2))
    for dy in range(3):
        for half in range(2):
            for x in range(2):
                for y in range(32):
                    source = (y + dy - 1) % 32
                    turn[dy, half, x, y, source // 2, half, x, source % 2] = 1
    add("turn_four", turn.reshape(384, 128))
    return np.concatenate(parts).astype(jnp.bfloat16), at


TABLE, AT = tables()


def mm(a, b):
    return jnp.dot(a, b, preferred_element_type=F32)


def mm_t(a, b):
    return lax.dot_general(a, b, (((1,), (1,)), ((), ())), preferred_element_type=F32)


def leaky(t):
    return jnp.maximum(t, 0.1 * t)


def rolled_64(v, back):
    lane = lax.broadcasted_iota(jnp.int32, v.shape, 1) % 64
    if back:
        return jnp.where(lane == 0, pltpu.roll(v, 65, 1), pltpu.roll(v, 1, 1))
    return jnp.where(lane == 63, pltpu.roll(v, 63, 1), pltpu.roll(v, 127, 1))


def kernel(
    feat, w2_in, b2_in, w3_in, b3_in, w4_in, b4_in, tab_in,
    out2, out3, out4,
    fx, fm, hs, hr, w2, w3, w4, b2, b3, b4, tab, wc2, z2, t2, wc3, z3, t3, bias2, bias3,
    pooled, own3, hs3, hr3, d3, l3, sa, rb, pp,
    load_sem, feat_sem, send_sem, recv_sem, send3_sem, recv3_sem, senda_sem, recva_sem, sendb_sem, recvb_sem,
):
    gx, gy = lax.axis_index("gx"), lax.axis_index("gy")
    xp, xm = lax.rem(gx + 1, 8), lax.rem(gx + 7, 8)
    yp, ym = lax.rem(gy + 1, 16), lax.rem(gy + 15, 16)

    def table(name, rows, lanes, skip=0):
        start = AT[name] + skip
        return tab[start : start + rows, :lanes]

    loads = [
        pltpu.make_async_copy(feat.at[:, x], fx.at[x + 1], feat_sem.at[x]) for x in range(8)
    ]
    others = [
        pltpu.make_async_copy(tab_in, tab, load_sem.at[0]),
        pltpu.make_async_copy(w2_in, w2, load_sem.at[1]),
        pltpu.make_async_copy(b2_in, b2, load_sem.at[2]),
        pltpu.make_async_copy(w3_in, w3, load_sem.at[3]),
        pltpu.make_async_copy(b3_in, b3, load_sem.at[4]),
        pltpu.make_async_copy(b4_in, b4, load_sem.at[5]),
        pltpu.make_async_copy(w4_in, w4.at[:, 0:3, :, 0:128], load_sem.at[6]),
        pltpu.make_async_copy(w4_in, w4.at[:, 1:4, :, 128:256], load_sem.at[7]),
    ]
    for copy in loads:
        copy.start()
    for copy in others:
        copy.start()

    barrier = pltpu.get_barrier_semaphore()

    def greet(x, y):
        pl.semaphore_signal(barrier, inc=1, device_id=(x, y), device_id_type=MESH)

    for x in (xm, xp):
        for y in (ym, yp):
            greet(x, y)
    for k in range(1, 16):
        greet(gx, lax.rem(gy + k, 16))
    for k in range(1, 8):
        greet(lax.rem(gx + k, 8), gy)
    pl.semaphore_wait(barrier, 4 + 15 + 7)

    def remote(src, dst, send, recv, x, y):
        return pltpu.make_async_remote_copy(
            src_ref=src, dst_ref=dst, send_sem=send, recv_sem=recv,
            device_id=(x, y), device_id_type=MESH,
        )

    first = [
        remote(feat.at[:, 7], fx.at[0], send_sem.at[0], recv_sem.at[0], xp, gy),
        remote(feat.at[:, 0], fx.at[9], send_sem.at[1], recv_sem.at[1], xm, gy),
    ]
    for copy in first:
        copy.start()

    def place(x):
        v = fx[x].astype(F32).reshape(256, 128)
        lanes = slice(x * 128, x * 128 + 128)
        fm[0:256, lanes] = pltpu.roll(v, 1, 1).astype(BF)
        fm[256:512, lanes] = v.astype(BF)
        fm[512:768, lanes] = pltpu.roll(v, 127, 1).astype(BF)

    for copy in loads:
        copy.wait()
    for x in range(1, 9):
        place(x)
    others[0].wait()
    edges = mm(table("select_two", 64, 256), fm[256:512, 128:1152]).astype(BF)
    for side in range(2):
        for x in range(8):
            hs[side, x] = edges[side * 32 : side * 32 + 32, x * 128 : x * 128 + 128]
    second = [
        remote(hs.at[1], hr.at[0, 1:9], send_sem.at[2], recv_sem.at[2], gx, yp),
        remote(hs.at[0], hr.at[1, 1:9], send_sem.at[3], recv_sem.at[3], gx, ym),
        remote(hs.at[1, 7], hr.at[0, 0], send_sem.at[4], recv_sem.at[4], xp, yp),
        remote(hs.at[1, 0], hr.at[0, 9], send_sem.at[5], recv_sem.at[5], xm, yp),
        remote(hs.at[0, 7], hr.at[1, 0], send_sem.at[6], recv_sem.at[6], xp, ym),
        remote(hs.at[0, 0], hr.at[1, 9], send_sem.at[7], recv_sem.at[7], xm, ym),
    ]
    for copy in second:
        copy.start()

    for copy in others[1:]:
        copy.wait()
    gap = jnp.zeros((32, 32), F32)
    for dx in range(3):
        for dz in range(3):
            k = 3 * dx + dz
            wc2[k * 32 : k * 32 + 32, :] = jnp.concatenate(
                [w2[9 * dx + 3 * dy + dz].astype(F32) for dy in range(3)] + [gap], axis=1
            ).astype(BF)
    for y in range(8):
        z2[:, y * 32 : y * 32 + 32, :] = (
            mm(wc2[...], table("spread_two", 128, 256, 128 * y)).astype(BF).reshape(9, 32, 256)
        )
    for dx in range(3):
        for dz in range(3):
            t2[dx, :, dz * 256 : dz * 256 + 256] = mm(
                table("order_two", 256, 256), z2[3 * dx + dz]
            ).astype(BF)
        low = [w2[9 * dx + dz].astype(F32) for dz in range(3)]
        high = [w2[9 * dx + 6 + dz].astype(F32) for dz in range(3)]
        z_edge = jnp.concatenate(
            [
                jnp.concatenate([low[0], gap, low[1], gap, low[2], gap, gap, gap], axis=1),
                jnp.concatenate([gap, high[0], gap, high[1], gap, high[2], gap, gap], axis=1),
            ],
            axis=0,
        ).astype(BF)
        t2[dx, :, 768:1024] = mm(table("edge_two", 256, 64), z_edge).astype(BF)
    row = lax.broadcasted_iota(jnp.int32, (256, 32), 0) // 8
    lane = lax.broadcasted_iota(jnp.int32, (256, 32), 1)
    column = jnp.sum(jnp.where(row == lane, b2[...], 0.0), axis=1, keepdims=True)
    bias2[...] = jnp.broadcast_to(column, (256, 128))

    for dx in range(3):
        for dz in range(3):
            k = 3 * dx + dz
            stack = jnp.concatenate(
                [w3[9 * dx + 3 * dy + dz] for dy in range(3)] + [jnp.zeros((32, 64), BF)], axis=0
            )
            wc3[k * 64 : k * 64 + 64, :] = mm_t(table("unit", 64, 64), stack).astype(BF)
    for y in range(4):
        z3[:, y * 64 : y * 64 + 64, :] = (
            mm(wc3[...], table("spread_three", 128, 128, 128 * y)).astype(BF).reshape(9, 64, 128)
        )
    gap = jnp.zeros((64, 32), F32)
    for dx in range(3):
        low, high = [], []
        for dz in range(3):
            k = 3 * dx + dz
            t3[dx, :, dz * 128 : dz * 128 + 128] = mm(table("order_three", 256, 256), z3[k]).astype(BF)
            block = wc3[k * 64 : k * 64 + 64, :].astype(F32)
            low.append(block[:, 0:32])
            high.append(block[:, 64:96])
        z_edge = jnp.concatenate(
            [
                jnp.concatenate([low[0], gap, low[1], gap, low[2], gap, gap, gap], axis=1),
                jnp.concatenate([gap, high[0], gap, high[1], gap, high[2], gap, gap], axis=1),
            ],
            axis=0,
        ).astype(BF)
        t3[dx, :, 384:640] = mm(table("edge_three", 256, 128), z_edge).astype(BF)
    row = lax.broadcasted_iota(jnp.int32, (256, 64), 0) // 4
    lane = lax.broadcasted_iota(jnp.int32, (256, 64), 1)
    column = jnp.sum(jnp.where(row == lane, b3[...], 0.0), axis=1, keepdims=True)
    bias3[...] = jnp.broadcast_to(column, (256, 128))

    w4[:, 3, :, 0:128] = jnp.zeros((9, 64, 128), BF)
    w4[:, 0, :, 128:256] = jnp.zeros((9, 64, 128), BF)

    fm[960:1024, :] = jnp.zeros((64, 1280), BF)
    for copy in first:
        copy.wait()
    place(0)
    place(9)
    for copy in second:
        copy.wait()
    for x in range(10):
        v = jnp.concatenate([hr[0, x], hr[1, x]], axis=0).astype(F32)
        lanes = slice(x * 128, x * 128 + 128)
        fm[768:832, lanes] = pltpu.roll(v, 1, 1).astype(BF)
        fm[832:896, lanes] = v.astype(BF)
        fm[896:960, lanes] = pltpu.roll(v, 127, 1).astype(BF)

    def quad(q, carry):
        total = jnp.zeros((256, 128), F32)
        for half in range(2):
            base = q * 4 + half * 2
            acc = jnp.zeros((256, 256), F32)
            for dx in range(3):
                lanes = pl.ds(pl.multiple_of((base + dx) * 128, 128), 256)
                acc = acc + mm(t2[dx], fm[:, lanes])
            bias = bias2[...]
            for x in range(2):
                v = leaky(acc[:, x * 128 : x * 128 + 128] + bias)
                out2[:, base + x] = v.reshape(32, 8, 128).astype(BF)
                total = total + mm(v.astype(BF), table("pool_two", 128, 128, half * 256 + x * 128))
        pooled[...] = total
        own3[q + 1] = (pooled[pl.ds(0, 128, stride=2), :] + pooled[pl.ds(1, 128, stride=2), :]).astype(BF)
        return carry

    lax.fori_loop(0, 2, quad, 0)

    for q in range(2):
        picked = mm(table("select_three", 64, 128), own3[q + 1]).astype(BF)
        hs3[0, q] = picked[0:32]
        hs3[1, q] = picked[32:64]
    third = [
        remote(own3.at[2], own3.at[0], send3_sem.at[0], recv3_sem.at[0], xp, gy),
        remote(own3.at[1], own3.at[3], send3_sem.at[1], recv3_sem.at[1], xm, gy),
        remote(hs3.at[1], hr3.at[0, 1:3], send3_sem.at[2], recv3_sem.at[2], gx, yp),
        remote(hs3.at[0], hr3.at[1, 1:3], send3_sem.at[3], recv3_sem.at[3], gx, ym),
        remote(hs3.at[1, 1], hr3.at[0, 0], send3_sem.at[4], recv3_sem.at[4], xp, yp),
        remote(hs3.at[1, 0], hr3.at[0, 3], send3_sem.at[5], recv3_sem.at[5], xm, yp),
        remote(hs3.at[0, 1], hr3.at[1, 0], send3_sem.at[6], recv3_sem.at[6], xp, ym),
        remote(hs3.at[0, 0], hr3.at[1, 3], send3_sem.at[7], recv3_sem.at[7], xm, ym),
    ]
    for copy in third:
        copy.start()
    d3[576:640, :] = jnp.zeros((64, 640), BF)
    for copy in third:
        copy.wait()
    tiles = []
    for t in range(4):
        tiles.append(
            jnp.concatenate([own3[t], hr3[0, t], hr3[1, t]], axis=0).astype(F32)
        )
    turned = [pltpu.roll(v, 64, 1) for v in tiles]
    lane = lax.broadcasted_iota(jnp.int32, (192, 128), 1)
    between = [jnp.where(lane < 64, turned[t], turned[t + 1]) for t in range(3)]
    for slot, v in enumerate([tiles[1], tiles[2]] + between):
        lanes = slice(slot * 128, slot * 128 + 128)
        for dz, u in enumerate((rolled_64(v, True), v, rolled_64(v, False))):
            u = u.astype(BF)
            d3[dz * 128 : dz * 128 + 128, lanes] = u[0:128]
            d3[384 + dz * 64 : 448 + dz * 64, lanes] = u[128:192]
    acc = mm(t3[0], d3[:, 256:512]) + mm(t3[1], d3[:, 0:256]) + mm(t3[2], d3[:, 384:640])
    for q in range(2):
        v = leaky(acc[:, q * 128 : q * 128 + 128] + bias3[...])
        l3[:, q * 128 : q * 128 + 128] = v.astype(BF)
        out3[:, 2 * q] = v[:, 0:64].reshape(64, 4, 64).astype(BF)
        out3[:, 2 * q + 1] = v[:, 64:128].reshape(64, 4, 64).astype(BF)

    sums = mm_t(table("pick_four", 256, 256), l3[...])
    row = lax.broadcasted_iota(jnp.int32, (256, 256), 0) % 2
    lane = lax.broadcasted_iota(jnp.int32, (256, 256), 1) % 4 // 2
    sums = jnp.where(row == lane, sums, 0.0)
    head = sums.astype(BF)
    tail = (sums - head.astype(F32)).astype(BF)
    block = jnp.zeros((128, 128), F32)
    for odd in range(2):
        g = table("gather_four", 256, 128, odd * 256)
        block = block + mm(head[odd * 128 : odd * 128 + 128], g) + mm(tail[odd * 128 : odd * 128 + 128], g)
    sa[...] = block.reshape(16, 8, 128).astype(BF)
    rb[gx, gy] = sa[gy]

    def send_a(k, carry):
        target = lax.rem(gy + k, 16)
        remote(sa.at[target], rb.at[gx, gy], senda_sem, recva_sem, gx, target).start()
        return carry

    lax.fori_loop(1, 16, send_a, 0)
    pltpu.make_async_copy(rb.at[gx, 0:15], rb.at[gx, 0:15], recva_sem).wait()

    def send_b(k, carry):
        target = lax.rem(gx + k, 8)
        remote(rb.at[gx], rb.at[gx], sendb_sem, recvb_sem, target, gy).start()
        return carry

    lax.fori_loop(1, 8, send_b, 0)
    pltpu.make_async_copy(sa.at[0:15], sa.at[0:15], senda_sem).wait()
    pltpu.make_async_copy(rb.at[0:7], rb.at[0:7], recvb_sem).wait()

    for x in range(8):
        v = rb[x].astype(F32).reshape(128, 128).astype(BF)
        moved = mm(table("turn_four", 384, 128), v).astype(BF)
        for dy in range(3):
            for half in range(2):
                start = (dy * 2 + half) * 64
                pp[dy, (1 + 2 * x) * 32 : (3 + 2 * x) * 32, half * 128 : half * 128 + 128] = moved[start : start + 64]
    pp[:, 0:32, :] = pp[:, 512:544, :]
    pp[:, 544:576, :] = pp[:, 32:64, :]
    bias = jnp.concatenate([b4[...], b4[...]], axis=1)

    def part(m, carry):
        acc = jnp.zeros((256, 256), F32)
        for dx in range(3):
            for dy in range(3):
                rows = pl.ds(pl.multiple_of(m * 256 + dx * 32, 32), 256)
                acc = acc + mm(pp[dy, rows, :], w4[3 * dx + dy].reshape(256, 256))
        v = leaky(acc + bias)
        out4[pl.ds(pl.multiple_of(m * 256, 256), 256)] = v.reshape(256, 2, 128).astype(BF)
        return carry

    lax.fori_loop(0, 2, part, 0)
    pltpu.make_async_copy(rb.at[0:7], rb.at[0:7], sendb_sem).wait()


def shards(features, weight_two, bias_two, weight_three, bias_three, weight_four, bias_four):
    vm = pl.BlockSpec(memory_space=pltpu.VMEM)
    hbm = pl.BlockSpec(memory_space=pl.ANY)
    table = jnp.asarray(TABLE)
    w3 = weight_three.transpose(0, 2, 1)
    w4 = weight_four.transpose(0, 2, 1).reshape(9, 3, 64, 128)
    dma = pltpu.SemaphoreType.DMA
    level_two, level_three, bottleneck = pl.pallas_call(
        kernel,
        out_shape=(
            jax.ShapeDtypeStruct((32, 8, 8, 128), BF),
            jax.ShapeDtypeStruct((64, 4, 4, 64), BF),
            jax.ShapeDtypeStruct((512, 2, 128), BF),
        ),
        in_specs=[hbm] * 8,
        out_specs=(vm, vm, vm),
        scratch_shapes=[
            pltpu.VMEM((10, 32, 8, 128), BF),
            pltpu.VMEM((1024, 1280), BF),
            pltpu.VMEM((2, 8, 32, 128), BF),
            pltpu.VMEM((2, 10, 32, 128), BF),
            pltpu.VMEM((27, 32, 32), BF),
            pltpu.VMEM((27, 32, 64), BF),
            pltpu.VMEM((9, 4, 64, 256), BF),
            pltpu.VMEM((1, 32), F32),
            pltpu.VMEM((1, 64), F32),
            pltpu.VMEM((1, 128), F32),
            pltpu.VMEM(TABLE.shape, BF),
            pltpu.VMEM((288, 128), BF),
            pltpu.VMEM((9, 256, 256), BF),
            pltpu.VMEM((3, 256, 1024), BF),
            pltpu.VMEM((576, 128), BF),
            pltpu.VMEM((9, 256, 128), BF),
            pltpu.VMEM((3, 256, 640), BF),
            pltpu.VMEM((256, 128), F32),
            pltpu.VMEM((256, 128), F32),
            pltpu.VMEM((256, 128), F32),
            pltpu.VMEM((4, 128, 128), BF),
            pltpu.VMEM((2, 2, 32, 128), BF),
            pltpu.VMEM((2, 4, 32, 128), BF),
            pltpu.VMEM((640, 640), BF),
            pltpu.VMEM((256, 256), BF),
            pltpu.VMEM((16, 8, 128), BF),
            pltpu.VMEM((8, 16, 8, 128), BF),
            pltpu.VMEM((3, 576, 256), BF),
            dma((8,)), dma((8,)), dma((8,)), dma((8,)), dma((8,)), dma((8,)),
            dma, dma, dma, dma,
        ],
        compiler_params=pltpu.CompilerParams(
            collective_id=0, has_side_effects=True, vmem_limit_bytes=40 * 1024 * 1024
        ),
    )(features, weight_two, bias_two[None], w3, bias_three[None], w4, bias_four[None], table)
    return level_two, level_three, bottleneck.reshape(16, 32, 2, 128).transpose(3, 0, 1, 2)


def solution(mesh):
    return jax.shard_map(
        shards,
        mesh=mesh,
        in_specs=(P(None, "gx", "gy", None), P(), P(), P(), P(), P(), P()),
        out_specs=(P(None, "gx", "gy", None), P(None, "gx", "gy", None), P(None, None, None, "gy")),
        check_vma=False,
    )
```

time: 118 us -> 48.2 us (0.41)
  the two profiles are of different devices: /device:TPU:1 before, /device:TPU:0 now
where the time goes in v1:
time: 48.2 us; the launch traced here: 47.9 us
  Pallas kernels  37.5 us (78%)
  local copies, waits for them, and re-layouts  9.72 us (20%)
  between operations  0.66 us (1%)
    pallas_call x1, Pallas kernels, shards(): pl.pallas_call(kernel, out_shape=(jax.ShapeDtypeStruct((32, 8, 8, 128), B...  37.5 us
    unnamed x19, local copies, waits for them, and re-layouts  9.72 us

profile of v1, /device:TPU:0, one launch (start us, length us, event | category | flops | bytes accessed | tf_op | source)
XLA Modules:
  0.0 47.9 jit_solution(15843606652382114222)
XLA Ops:
  0.6 0.0 copy-start
  0.6 1.6 %copy-done = bf16[4416,256]{1,0:T(8,128)(2,1)S(1)} copy-done((bf16[4416,256]{1,0:T(8,128)(2,1)S(1)}, bf16[4416,256]{1,0:T(8,128)(2,1)}, u32[]{:S(2)}) %copy-start) | copy-done | bytes 2261016
  2.3 0.0 copy-start.1
  2.3 1.0 %copy-done.1 = bf16[32,8,8,128]{3,2,1,0:T(8,128)(2,1)S(1)} copy-done((bf16[32,8,8,128]{3,2,1,0:T(8,128)(2,1)S(1)}, bf16[32,8,8,128]{3,2,1,0:T(8,128)(2,1)}, u32[]{:S(2)}) %copy-start.1) | copy-done | bytes 524312
  3.3 0.0 copy-start.2
  3.3 1.0 %copy-done.2 = bf16[27,128,64]{1,2,0:T(8,128)(2,1)S(1)} copy-done((bf16[27,128,64]{1,2,0:T(8,128)(2,1)S(1)}, bf16[27,128,64]{1,2,0:T(8,128)(2,1)}, u32[]{:S(2)}) %copy-start.2) | copy-done | bytes 442392
  4.3 0.0 copy-start.3
  4.3 0.9 %copy-done.3 = bf16[27,32,32]{2,1,0:T(8,128)(2,1)S(1)} copy-done((bf16[27,32,32]{2,1,0:T(8,128)(2,1)S(1)}, bf16[27,32,32]{2,1,0:T(8,128)(2,1)}, u32[]{:S(2)}) %copy-start.3) | copy-done | bytes 55320
  5.3 0.0 copy-start.4
  5.3 0.9 %copy-done.4 = bf16[27,64,32]{1,2,0:T(8,128)(2,1)S(1)} copy-done((bf16[27,64,32]{1,2,0:T(8,128)(2,1)S(1)}, bf16[27,64,32]{1,2,0:T(8,128)(2,1)}, u32[]{:S(2)}) %copy-start.4) | copy-done | bytes 110616
  6.2 0.0 copy-start.5
  6.2 0.7 %copy-done.5 = f32[32]{0:T(128)S(1)} copy-done((f32[32]{0:T(128)S(1)}, f32[32]{0:T(128)}, u32[]{:S(2)}) %copy-start.5) | copy-done | bytes 152
  6.9 0.0 copy-start.6
  6.9 0.7 %copy-done.6 = f32[64]{0:T(128)S(1)} copy-done((f32[64]{0:T(128)S(1)}, f32[64]{0:T(128)}, u32[]{:S(2)}) %copy-start.6) | copy-done | bytes 280
  7.5 0.0 copy-start.7
  7.5 0.7 %copy-done.7 = f32[128]{0:T(128)S(1)} copy-done((f32[128]{0:T(128)S(1)}, f32[128]{0:T(128)}, u32[]{:S(2)}) %copy-start.7) | copy-done | bytes 536
  8.2 37.5 %shard_map.103 = (bf16[32,8,8,128]{3,2,1,0:T(8,128)(2,1)S(1)}, bf16[64,4,4,64]{3,2,1,0:T(4,128)(2,1)S(1)}, bf16[512,2,128]{2,1,0:T(2,128)(2,1)S(1)}) custom-call(bf16[32,8,8,128]{3,2,1,0:T(8,128)(2,1)S(1)} %copy-done.1, bf16[27,32,32]{2,1,0:T(8,128)(2,1)S(1)} %copy-done.3, f32[1,32]{1,0:T(1,128)S(1)} %bitcast.13, bf16[27,32,64]{2,1,0:T(8,128)(2,1)S(1)} %bitcast.12, ...), custom_call_target="tpu_custom_call" | custom-call | tf_op jit(solution)/shard_map/pallas_call | solution.py:416
  45.7 0.8 %copy.14 = bf16[32,8,8,128]{3,2,1,0:T(8,128)(2,1)} copy(bf16[32,8,8,128]{3,2,1,0:T(8,128)(2,1)S(1)} %get-tuple-element.12) | data formatting | bytes 1048576
  46.5 0.7 %copy.15 = bf16[64,4,4,64]{3,2,1,0:T(4,128)(2,1)} copy(bf16[64,4,4,64]{3,2,1,0:T(4,128)(2,1)S(1)} %get-tuple-element.13) | data formatting | bytes 262144
  47.2 0.7 %copy.16 = bf16[128,16,32,2]{0,3,2,1:T(2,128)(2,1)} copy(bf16[128,16,32,2]{0,3,2,1:T(2,128)(2,1)S(1)} %bitcast.11) | data formatting | bytes 524288
Async XLA Ops:
  0.6 1.6 %copy-start = (bf16[4416,256]{1,0:T(8,128)(2,1)S(1)}, bf16[4416,256]{1,0:T(8,128)(2,1)}, u32[]{:S(2)}) copy-start(bf16[4416,256]{1,0:T(8,128)(2,1)} %constant.2.clone.tab_in) | copy-start | bytes 6782980
  2.3 1.0 %copy-start.1 = (bf16[32,8,8,128]{3,2,1,0:T(8,128)(2,1)S(1)}, bf16[32,8,8,128]{3,2,1,0:T(8,128)(2,1)}, u32[]{:S(2)}) copy-start(bf16[32,8,8,128]{3,2,1,0:T(8,128)(2,1)} %feat.1) | copy-start | bytes 1572868
  3.3 1.0 %copy-start.2 = (bf16[27,128,64]{1,2,0:T(8,128)(2,1)S(1)}, bf16[27,128,64]{1,2,0:T(8,128)(2,1)}, u32[]{:S(2)}) copy-start(bf16[27,128,64]{1,2,0:T(8,128)(2,1)} %param.13) | copy-start | bytes 1327108
  4.3 0.9 %copy-start.3 = (bf16[27,32,32]{2,1,0:T(8,128)(2,1)S(1)}, bf16[27,32,32]{2,1,0:T(8,128)(2,1)}, u32[]{:S(2)}) copy-start(bf16[27,32,32]{2,1,0:T(8,128)(2,1)} %w2_in.1) | copy-start | bytes 165892
  5.3 0.9 %copy-start.4 = (bf16[27,64,32]{1,2,0:T(8,128)(2,1)S(1)}, bf16[27,64,32]{1,2,0:T(8,128)(2,1)}, u32[]{:S(2)}) copy-start(bf16[27,64,32]{1,2,0:T(8,128)(2,1)} %param.11) | copy-start | bytes 331780
  6.2 0.7 %copy-start.5 = (f32[32]{0:T(128)S(1)}, f32[32]{0:T(128)}, u32[]{:S(2)}) copy-start(f32[32]{0:T(128)} %param.10) | copy-start | bytes 388
  6.9 0.7 %copy-start.6 = (f32[64]{0:T(128)S(1)}, f32[64]{0:T(128)}, u32[]{:S(2)}) copy-start(f32[64]{0:T(128)} %param.12) | copy-start | bytes 772
  7.5 0.7 %copy-start.7 = (f32[128]{0:T(128)S(1)}, f32[128]{0:T(128)}, u32[]{:S(2)}) copy-start(f32[128]{0:T(128)} %param.14) | copy-start | bytes 1540

commit v2 on v1

--- a/solution.py
+++ b/solution.py
@@ -25,11 +25,6 @@
         parts.append(full)
         row += full.shape[0]
 
-    select = np.zeros((64, 256))
-    for c in range(32):
-        select[c, c * 8] = 1
-        select[32 + c, c * 8 + 7] = 1
-    add("select_two", select)
     spread = np.zeros((8, 128, 256))
     for y in range(8):
         for dy in range(3):
@@ -124,9 +119,9 @@
 
 def kernel(
     feat, w2_in, b2_in, w3_in, b3_in, w4_in, b4_in, tab_in,
-    out2, out3, out4,
-    fx, fm, hs, hr, w2, w3, w4, b2, b3, b4, tab, wc2, z2, t2, wc3, z3, t3, bias2, bias3,
-    pooled, own3, hs3, hr3, d3, l3, sa, rb, pp,
+    out2, out3, rb, w4, turn, b4,
+    fx, fm, hs, hr, w2, w3, b2, b3, tab, wc2, z2, t2, a2, wc3, z3, t3, bias2, bias3,
+    pooled, own3, hs3, hr3, d3, l3, sa,
     load_sem, feat_sem, send_sem, recv_sem, send3_sem, recv3_sem, senda_sem, recva_sem, sendb_sem, recvb_sem,
 ):
     gx, gy = lax.axis_index("gx"), lax.axis_index("gy")
@@ -137,6 +132,18 @@
         start = AT[name] + skip
         return tab[start : start + rows, :lanes]
 
+    barrier = pltpu.get_barrier_semaphore()
+
+    def greet(x, y):
+        pl.semaphore_signal(barrier, inc=1, device_id=(x, y), device_id_type=MESH)
+
+    for x in (xm, xp):
+        for y in (ym, yp):
+            greet(x, y)
+    for k in range(1, 16):
+        greet(gx, lax.rem(gy + k, 16))
+    for k in range(1, 8):
+        greet(lax.rem(gx + k, 8), gy)
     loads = [
         pltpu.make_async_copy(feat.at[:, x], fx.at[x + 1], feat_sem.at[x]) for x in range(8)
     ]
@@ -155,18 +162,6 @@
     for copy in others:
         copy.start()
 
-    barrier = pltpu.get_barrier_semaphore()
-
-    def greet(x, y):
-        pl.semaphore_signal(barrier, inc=1, device_id=(x, y), device_id_type=MESH)
-
-    for x in (xm, xp):
-        for y in (ym, yp):
-            greet(x, y)
-    for k in range(1, 16):
-        greet(gx, lax.rem(gy + k, 16))
-    for k in range(1, 8):
-        greet(lax.rem(gx + k, 8), gy)
     pl.semaphore_wait(barrier, 4 + 15 + 7)
 
     def remote(src, dst, send, recv, x, y):
@@ -185,31 +180,39 @@
     def place(x):
         v = fx[x].astype(F32).reshape(256, 128)
         lanes = slice(x * 128, x * 128 + 128)
+        fm[256:512, lanes] = v.astype(BF)
+
+    def shift(x):
+        lanes = slice(x * 128, x * 128 + 128)
+        v = fm[256:512, lanes].astype(F32)
         fm[0:256, lanes] = pltpu.roll(v, 1, 1).astype(BF)
-        fm[256:512, lanes] = v.astype(BF)
         fm[512:768, lanes] = pltpu.roll(v, 127, 1).astype(BF)
 
+    row = lax.broadcasted_iota(jnp.int32, (64, 256), 0)
+    lane = lax.broadcasted_iota(jnp.int32, (64, 256), 1)
+    select = jnp.where(lane == row % 32 * 8 + row // 32 * 7, 1.0, 0.0).astype(BF)
     for copy in loads:
         copy.wait()
     for x in range(1, 9):
         place(x)
-    others[0].wait()
-    edges = mm(table("select_two", 64, 256), fm[256:512, 128:1152]).astype(BF)
+    edges = mm(select, fm[256:512, 128:1152]).astype(BF)
     for side in range(2):
         for x in range(8):
             hs[side, x] = edges[side * 32 : side * 32 + 32, x * 128 : x * 128 + 128]
     second = [
-        remote(hs.at[1], hr.at[0, 1:9], send_sem.at[2], recv_sem.at[2], gx, yp),
-        remote(hs.at[0], hr.at[1, 1:9], send_sem.at[3], recv_sem.at[3], gx, ym),
         remote(hs.at[1, 7], hr.at[0, 0], send_sem.at[4], recv_sem.at[4], xp, yp),
         remote(hs.at[1, 0], hr.at[0, 9], send_sem.at[5], recv_sem.at[5], xm, yp),
         remote(hs.at[0, 7], hr.at[1, 0], send_sem.at[6], recv_sem.at[6], xp, ym),
         remote(hs.at[0, 0], hr.at[1, 9], send_sem.at[7], recv_sem.at[7], xm, ym),
+        remote(hs.at[1], hr.at[0, 1:9], send_sem.at[2], recv_sem.at[2], gx, yp),
+        remote(hs.at[0], hr.at[1, 1:9], send_sem.at[3], recv_sem.at[3], gx, ym),
     ]
     for copy in second:
         copy.start()
 
-    for copy in others[1:]:
+    for x in range(1, 9):
+        shift(x)
+    for copy in others:
         copy.wait()
     gap = jnp.zeros((32, 32), F32)
     for dx in range(3):
@@ -277,12 +280,29 @@
 
     w4[:, 3, :, 0:128] = jnp.zeros((9, 64, 128), BF)
     w4[:, 0, :, 128:256] = jnp.zeros((9, 64, 128), BF)
-
+    turn[...] = table("turn_four", 384, 128)
+
+    fm[0:768, 0:128] = jnp.zeros((768, 128), BF)
+    fm[0:768, 1152:1280] = jnp.zeros((768, 128), BF)
     fm[960:1024, :] = jnp.zeros((64, 1280), BF)
+
+    def inner(p, carry):
+        acc = jnp.zeros((256, 256), F32)
+        for dx in range(3):
+            lanes = pl.ds(pl.multiple_of((p * 2 + dx) * 128, 128), 256)
+            acc = acc + mm(t2[dx, :, 0:768], fm[0:768, lanes])
+        a2[p] = acc
+        return carry
+
+    lax.fori_loop(0, 4, inner, 0)
+
     for copy in first:
         copy.wait()
-    place(0)
-    place(9)
+    for x in (0, 9):
+        place(x)
+        shift(x)
+    a2[0, :, 0:128] += mm(t2[0, :, 0:768], fm[0:768, 0:128])
+    a2[3, :, 128:256] += mm(t2[2, :, 0:768], fm[0:768, 1152:1280])
     for copy in second:
         copy.wait()
     for x in range(10):
@@ -292,41 +312,36 @@
         fm[832:896, lanes] = v.astype(BF)
         fm[896:960, lanes] = pltpu.roll(v, 127, 1).astype(BF)
 
-    def quad(q, carry):
+    third = []
+    for q in range(2):
         total = jnp.zeros((256, 128), F32)
         for half in range(2):
-            base = q * 4 + half * 2
-            acc = jnp.zeros((256, 256), F32)
+            p = 2 * q + half
+            acc = a2[p]
             for dx in range(3):
-                lanes = pl.ds(pl.multiple_of((base + dx) * 128, 128), 256)
-                acc = acc + mm(t2[dx], fm[:, lanes])
-            bias = bias2[...]
+                lanes = slice((p * 2 + dx) * 128, (p * 2 + dx + 2) * 128)
+                acc = acc + mm(t2[dx, :, 768:1024], fm[768:1024, lanes])
             for x in range(2):
-                v = leaky(acc[:, x * 128 : x * 128 + 128] + bias)
-                out2[:, base + x] = v.reshape(32, 8, 128).astype(BF)
+                v = leaky(acc[:, x * 128 : x * 128 + 128] + bias2[...])
+                out2[:, 2 * p + x] = v.reshape(32, 8, 128).astype(BF)
                 total = total + mm(v.astype(BF), table("pool_two", 128, 128, half * 256 + x * 128))
         pooled[...] = total
         own3[q + 1] = (pooled[pl.ds(0, 128, stride=2), :] + pooled[pl.ds(1, 128, stride=2), :]).astype(BF)
-        return carry
-
-    lax.fori_loop(0, 2, quad, 0)
-
-    for q in range(2):
+        far, slot = (xm, 3) if q == 0 else (xp, 0)
+        base = 5 * q
         picked = mm(table("select_three", 64, 128), own3[q + 1]).astype(BF)
         hs3[0, q] = picked[0:32]
         hs3[1, q] = picked[32:64]
-    third = [
-        remote(own3.at[2], own3.at[0], send3_sem.at[0], recv3_sem.at[0], xp, gy),
-        remote(own3.at[1], own3.at[3], send3_sem.at[1], recv3_sem.at[1], xm, gy),
-        remote(hs3.at[1], hr3.at[0, 1:3], send3_sem.at[2], recv3_sem.at[2], gx, yp),
-        remote(hs3.at[0], hr3.at[1, 1:3], send3_sem.at[3], recv3_sem.at[3], gx, ym),
-        remote(hs3.at[1, 1], hr3.at[0, 0], send3_sem.at[4], recv3_sem.at[4], xp, yp),
-        remote(hs3.at[1, 0], hr3.at[0, 3], send3_sem.at[5], recv3_sem.at[5], xm, yp),
-        remote(hs3.at[0, 1], hr3.at[1, 0], send3_sem.at[6], recv3_sem.at[6], xp, ym),
-        remote(hs3.at[0, 0], hr3.at[1, 3], send3_sem.at[7], recv3_sem.at[7], xm, ym),
-    ]
-    for copy in third:
-        copy.start()
+        copies = [
+            remote(hs3.at[1, q], hr3.at[0, slot], send3_sem.at[base], recv3_sem.at[base], far, yp),
+            remote(hs3.at[0, q], hr3.at[1, slot], send3_sem.at[base + 1], recv3_sem.at[base + 1], far, ym),
+            remote(own3.at[q + 1], own3.at[slot], send3_sem.at[base + 2], recv3_sem.at[base + 2], far, gy),
+            remote(hs3.at[1, q], hr3.at[0, q + 1], send3_sem.at[base + 3], recv3_sem.at[base + 3], gx, yp),
+            remote(hs3.at[0, q], hr3.at[1, q + 1], send3_sem.at[base + 4], recv3_sem.at[base + 4], gx, ym),
+        ]
+        for copy in copies:
+            copy.start()
+        third += copies
     d3[576:640, :] = jnp.zeros((64, 640), BF)
     for copy in third:
         copy.wait()
@@ -381,9 +396,19 @@
     pltpu.make_async_copy(sa.at[0:15], sa.at[0:15], senda_sem).wait()
     pltpu.make_async_copy(rb.at[0:7], rb.at[0:7], recvb_sem).wait()
 
+    pltpu.make_async_copy(rb.at[0:7], rb.at[0:7], sendb_sem).wait()
+
+
+def last(out2_in, out3_in, rb, w4, turn, b4, out2, out3, out4, pp, l4, sem):
+    leaving = [
+        pltpu.make_async_copy(out2_in, out2, sem.at[0]),
+        pltpu.make_async_copy(out3_in, out3, sem.at[1]),
+    ]
+    for copy in leaving:
+        copy.start()
     for x in range(8):
         v = rb[x].astype(F32).reshape(128, 128).astype(BF)
-        moved = mm(table("turn_four", 384, 128), v).astype(BF)
+        moved = mm(turn[...], v).astype(BF)
         for dy in range(3):
             for half in range(2):
                 start = (dy * 2 + half) * 64
@@ -391,37 +416,40 @@
     pp[:, 0:32, :] = pp[:, 512:544, :]
     pp[:, 544:576, :] = pp[:, 32:64, :]
     bias = jnp.concatenate([b4[...], b4[...]], axis=1)
-
-    def part(m, carry):
+    for m in range(2):
         acc = jnp.zeros((256, 256), F32)
         for dx in range(3):
             for dy in range(3):
-                rows = pl.ds(pl.multiple_of(m * 256 + dx * 32, 32), 256)
+                rows = slice(m * 256 + dx * 32, m * 256 + dx * 32 + 256)
                 acc = acc + mm(pp[dy, rows, :], w4[3 * dx + dy].reshape(256, 256))
         v = leaky(acc + bias)
-        out4[pl.ds(pl.multiple_of(m * 256, 256), 256)] = v.reshape(256, 2, 128).astype(BF)
-        return carry
-
-    lax.fori_loop(0, 2, part, 0)
-    pltpu.make_async_copy(rb.at[0:7], rb.at[0:7], sendb_sem).wait()
+        l4[m * 256 : m * 256 + 256] = v.reshape(256, 2, 128).astype(BF)
+        piece = pl.ds(m * 256, 256)
+        leaving.append(pltpu.make_async_copy(l4.at[piece], out4.at[piece], sem.at[2 + m]))
+        leaving[-1].start()
+    for copy in leaving:
+        copy.wait()
 
 
 def shards(features, weight_two, bias_two, weight_three, bias_three, weight_four, bias_four):
     vm = pl.BlockSpec(memory_space=pltpu.VMEM)
-    hbm = pl.BlockSpec(memory_space=pl.ANY)
+    hbm = pl.BlockSpec(memory_space=pltpu.HBM)
     table = jnp.asarray(TABLE)
     w3 = weight_three.transpose(0, 2, 1)
     w4 = weight_four.transpose(0, 2, 1).reshape(9, 3, 64, 128)
     dma = pltpu.SemaphoreType.DMA
-    level_two, level_three, bottleneck = pl.pallas_call(
+    held = pl.pallas_call(
         kernel,
         out_shape=(
             jax.ShapeDtypeStruct((32, 8, 8, 128), BF),
             jax.ShapeDtypeStruct((64, 4, 4, 64), BF),
-            jax.ShapeDtypeStruct((512, 2, 128), BF),
+            jax.ShapeDtypeStruct((8, 16, 8, 128), BF),
+            jax.ShapeDtypeStruct((9, 4, 64, 256), BF),
+            jax.ShapeDtypeStruct((384, 128), BF),
+            jax.ShapeDtypeStruct((1, 128), F32),
         ),
         in_specs=[hbm] * 8,
-        out_specs=(vm, vm, vm),
+        out_specs=(vm,) * 6,
         scratch_shapes=[
             pltpu.VMEM((10, 32, 8, 128), BF),
             pltpu.VMEM((1024, 1280), BF),
@@ -429,14 +457,13 @@
             pltpu.VMEM((2, 10, 32, 128), BF),
             pltpu.VMEM((27, 32, 32), BF),
             pltpu.VMEM((27, 32, 64), BF),
-            pltpu.VMEM((9, 4, 64, 256), BF),
             pltpu.VMEM((1, 32), F32),
             pltpu.VMEM((1, 64), F32),
-            pltpu.VMEM((1, 128), F32),
             pltpu.VMEM(TABLE.shape, BF),
             pltpu.VMEM((288, 128), BF),
             pltpu.VMEM((9, 256, 256), BF),
             pltpu.VMEM((3, 256, 1024), BF),
+            pltpu.VMEM((4, 256, 256), F32),
             pltpu.VMEM((576, 128), BF),
             pltpu.VMEM((9, 256, 128), BF),
             pltpu.VMEM((3, 256, 640), BF),
@@ -449,15 +476,34 @@
             pltpu.VMEM((640, 640), BF),
             pltpu.VMEM((256, 256), BF),
             pltpu.VMEM((16, 8, 128), BF),
-            pltpu.VMEM((8, 16, 8, 128), BF),
-            pltpu.VMEM((3, 576, 256), BF),
-            dma((8,)), dma((8,)), dma((8,)), dma((8,)), dma((8,)), dma((8,)),
+            dma((8,)), dma((8,)), dma((8,)), dma((8,)), dma((10,)), dma((10,)),
             dma, dma, dma, dma,
         ],
         compiler_params=pltpu.CompilerParams(
             collective_id=0, has_side_effects=True, vmem_limit_bytes=40 * 1024 * 1024
         ),
-    )(features, weight_two, bias_two[None], w3, bias_three[None], w4, bias_four[None], table)
+    )(
+        *(
+            pltpu.with_memory_space_constraint(a, pltpu.HBM)
+            for a in (features, weight_two, bias_two[None], w3, bias_three[None], w4, bias_four[None], table)
+        )
+    )
+    level_two, level_three, bottleneck = pl.pallas_call(
+        last,
+        out_shape=(
+            jax.ShapeDtypeStruct((32, 8, 8, 128), BF),
+            jax.ShapeDtypeStruct((64, 4, 4, 64), BF),
+            jax.ShapeDtypeStruct((512, 2, 128), BF),
+        ),
+        in_specs=[vm] * 6,
+        out_specs=(hbm,) * 3,
+        scratch_shapes=[
+            pltpu.VMEM((3, 576, 256), BF),
+            pltpu.VMEM((512, 2, 128), BF),
+            dma((4,)),
+        ],
+        compiler_params=pltpu.CompilerParams(vmem_limit_bytes=40 * 1024 * 1024),
+    )(*held)
     return level_two, level_three, bottleneck.reshape(16, 32, 2, 128).transpose(3, 0, 1, 2)
 
 

time: 48.2 us -> 35.5 us (0.74)
  the two profiles are of different devices: /device:TPU:0 before, /device:TPU:1 now
where the time goes in v2:
time: 35.5 us; the launch traced here: 35.4 us
  Pallas kernels  34.7 us (98%)
  between operations  0.64 us (2%)
    pallas_call x1, Pallas kernels, shards(): pl.pallas_call(kernel, out_shape=(jax.ShapeDtypeStruct((32, 8, 8, 128), B...  32.7 us
    pallas_call x1, Pallas kernels, shards(): pl.pallas_call(last, out_shape=(jax.ShapeDtypeStruct((32, 8, 8, 128), BF)...  2.02 us

profile of v2, /device:TPU:1, one launch (start us, length us, event | category | flops | bytes accessed | tf_op | source)
XLA Modules:
  0.0 35.4 jit_solution(15736961899579980704)
XLA Ops:
  0.6 32.7 %shard_map.103 = (bf16[32,8,8,128]{3,2,1,0:T(8,128)(2,1)S(1)}, bf16[64,4,4,64]{3,2,1,0:T(4,128)(2,1)S(1)}, bf16[8,16,8,128]{3,2,1,0:T(8,128)(2,1)S(1)}, bf16[9,4...) custom-call(bf16[32,8,8,128]{3,2,1,0:T(8,128)(2,1)} %feat.1, ...), custom_call_target="tpu_custom_call" | custom-call | tf_op jit(solution)/shard_map/pallas_call | solution.py:441
  33.4 2.0 %shard_map.104 = (bf16[32,8,8,128]{3,2,1,0:T(8,128)(2,1)}, bf16[64,4,4,64]{3,2,1,0:T(4,128)(2,1)}, bf16[512,2,128]{2,1,0:T(2,128)(2,1)}) custom-call(bf16[32,8,8,128]{3,2,1,0:T(8,128)(2,1)S(1)} %get-tuple-element.12.out2_in, bf16[64,4,4,64]{3,2,1,0:T(4,128)(2,1)S(1)} %get-tuple-element.13.out3_in, bf16[8,16,8,128]{3,2,1,0:T(8,128)(2,1)S(1)} %get-tuple-element.14.rb, ...), custom_call_target="tpu_custom_call" | custom-call | tf_op jit(solution)/shard_map/pallas_call | solution.py:491

commit v3 on v2

--- a/solution.py
+++ b/solution.py
@@ -122,7 +122,7 @@
     out2, out3, rb, w4, turn, b4,
     fx, fm, hs, hr, w2, w3, b2, b3, tab, wc2, z2, t2, a2, wc3, z3, t3, bias2, bias3,
     pooled, own3, hs3, hr3, d3, l3, sa,
-    load_sem, feat_sem, send_sem, recv_sem, send3_sem, recv3_sem, senda_sem, recva_sem, sendb_sem, recvb_sem,
+    load_sem, feat_sem, send_sem, recv_sem, send3_sem, recv3_sem, senda_sem, recva_sem, wide_sem,
 ):
     gx, gy = lax.axis_index("gx"), lax.axis_index("gy")
     xp, xm = lax.rem(gx + 1, 8), lax.rem(gx + 7, 8)
@@ -134,16 +134,15 @@
 
     barrier = pltpu.get_barrier_semaphore()
 
-    def greet(x, y):
-        pl.semaphore_signal(barrier, inc=1, device_id=(x, y), device_id_type=MESH)
-
-    for x in (xm, xp):
-        for y in (ym, yp):
-            greet(x, y)
-    for k in range(1, 16):
-        greet(gx, lax.rem(gy + k, 16))
-    for k in range(1, 8):
-        greet(lax.rem(gx + k, 8), gy)
+    def greet(semaphore, dx, dy):
+        pl.semaphore_signal(
+            semaphore, inc=1, device_id=(lax.rem(gx + dx + 8, 8), lax.rem(gy + dy + 16, 16)), device_id_type=MESH
+        )
+
+    around = [(dx, dy) for dx in (-1, 0, 1) for dy in (-1, 0, 1) if dx or dy]
+    for dx, dy in around:
+        greet(barrier, dx, dy)
+
     loads = [
         pltpu.make_async_copy(feat.at[:, x], fx.at[x + 1], feat_sem.at[x]) for x in range(8)
     ]
@@ -162,7 +161,7 @@
     for copy in others:
         copy.start()
 
-    pl.semaphore_wait(barrier, 4 + 15 + 7)
+    pl.semaphore_wait(barrier, 8)
 
     def remote(src, dst, send, recv, x, y):
         return pltpu.make_async_remote_copy(
@@ -210,6 +209,8 @@
     for copy in second:
         copy.start()
 
+    for dx, dy in around:
+        greet(wide_sem.at[0], dx, dy)
     for x in range(1, 9):
         shift(x)
     for copy in others:
@@ -245,6 +246,10 @@
     column = jnp.sum(jnp.where(row == lane, b2[...], 0.0), axis=1, keepdims=True)
     bias2[...] = jnp.broadcast_to(column, (256, 128))
 
+    pl.semaphore_wait(wide_sem.at[0], 8)
+    for dx, dy in around:
+        greet(wide_sem.at[1], 2 * dx, 2 * dy)
+
     for dx in range(3):
         for dz in range(3):
             k = 3 * dx + dz
@@ -281,6 +286,10 @@
     w4[:, 3, :, 0:128] = jnp.zeros((9, 64, 128), BF)
     w4[:, 0, :, 128:256] = jnp.zeros((9, 64, 128), BF)
     turn[...] = table("turn_four", 384, 128)
+
+    pl.semaphore_wait(wide_sem.at[1], 8)
+    for dy in (-4, 4):
+        greet(wide_sem.at[2], 0, dy)
 
     fm[0:768, 0:128] = jnp.zeros((768, 128), BF)
     fm[0:768, 1152:1280] = jnp.zeros((768, 128), BF)
@@ -377,26 +386,27 @@
         g = table("gather_four", 256, 128, odd * 256)
         block = block + mm(head[odd * 128 : odd * 128 + 128], g) + mm(tail[odd * 128 : odd * 128 + 128], g)
     sa[...] = block.reshape(16, 8, 128).astype(BF)
-    rb[gx, gy] = sa[gy]
-
-    def send_a(k, carry):
-        target = lax.rem(gy + k, 16)
-        remote(sa.at[target], rb.at[gx, gy], senda_sem, recva_sem, gx, target).start()
-        return carry
-
-    lax.fori_loop(1, 16, send_a, 0)
-    pltpu.make_async_copy(rb.at[gx, 0:15], rb.at[gx, 0:15], recva_sem).wait()
-
-    def send_b(k, carry):
-        target = lax.rem(gx + k, 8)
-        remote(rb.at[gx], rb.at[gx], sendb_sem, recvb_sem, target, gy).start()
-        return carry
-
-    lax.fori_loop(1, 8, send_b, 0)
-    pltpu.make_async_copy(sa.at[0:15], sa.at[0:15], senda_sem).wait()
-    pltpu.make_async_copy(rb.at[0:7], rb.at[0:7], recvb_sem).wait()
-
-    pltpu.make_async_copy(rb.at[0:7], rb.at[0:7], sendb_sem).wait()
+    pl.semaphore_wait(wide_sem.at[2], 2)
+    me = gx * 16 + gy
+    mine = pltpu.make_async_copy(sa.at[gy], rb.at[me], recva_sem)
+    y_at, x_at, z_at, core_at = gx // 4 * 2 + gy // 8, gx % 4, gy // 2 % 4, gy % 2
+    columns, layers = {}, {}
+    for d in range(4):
+        y = (y_at + d) % 4
+        for e in range(4):
+            columns[e, d] = y // 2 * 4 + (x_at + e) % 4
+            layers[d, e] = y % 2 * 8 + (z_at + e) % 4 * 2
+    hops = (0, 1, 2, 1)
+    steps = [(dx, dy, dz) for dx in range(4) for dy in range(4) for dz in range(4)]
+    steps.sort(key=lambda step: -sum(hops[d] for d in step))
+    for dx, dy, dz in steps:
+        for flip in range(2):
+            if dx or dy or dz or flip:
+                layer = layers[dy, dz] + (core_at + flip) % 2
+                remote(sa.at[layer], rb.at[me], senda_sem, recva_sem, columns[dx, dy], layer).start()
+    mine.start()
+    pltpu.make_async_copy(rb, rb, recva_sem).wait()
+    pltpu.make_async_copy(rb.at[0:127], rb.at[0:127], senda_sem).wait()
 
 
 def last(out2_in, out3_in, rb, w4, turn, b4, out2, out3, out4, pp, l4, sem):
@@ -407,7 +417,7 @@
     for copy in leaving:
         copy.start()
     for x in range(8):
-        v = rb[x].astype(F32).reshape(128, 128).astype(BF)
+        v = rb[x * 16 : x * 16 + 16].astype(F32).reshape(128, 128).astype(BF)
         moved = mm(turn[...], v).astype(BF)
         for dy in range(3):
             for half in range(2):
@@ -443,7 +453,7 @@
         out_shape=(
             jax.ShapeDtypeStruct((32, 8, 8, 128), BF),
             jax.ShapeDtypeStruct((64, 4, 4, 64), BF),
-            jax.ShapeDtypeStruct((8, 16, 8, 128), BF),
+            jax.ShapeDtypeStruct((128, 8, 128), BF),
             jax.ShapeDtypeStruct((9, 4, 64, 256), BF),
             jax.ShapeDtypeStruct((384, 128), BF),
             jax.ShapeDtypeStruct((1, 128), F32),
@@ -477,7 +487,7 @@
             pltpu.VMEM((256, 256), BF),
             pltpu.VMEM((16, 8, 128), BF),
             dma((8,)), dma((8,)), dma((8,)), dma((8,)), dma((10,)), dma((10,)),
-            dma, dma, dma, dma,
+            dma, dma, pltpu.SemaphoreType.REGULAR((3,)),
         ],
         compiler_params=pltpu.CompilerParams(
             collective_id=0, has_side_effects=True, vmem_limit_bytes=40 * 1024 * 1024

time: 35.5 us -> 35.4 us (level)
  no operation moved by 1% of the time
where the time goes in v3:
time: 35.4 us; the launch traced here: 35.2 us
  Pallas kernels  34.6 us (98%)
  between operations  0.64 us (2%)
    pallas_call x1, Pallas kernels, shards(): pl.pallas_call(kernel, out_shape=(jax.ShapeDtypeStruct((32, 8, 8, 128), B...  32.6 us
    pallas_call x1, Pallas kernels, shards(): pl.pallas_call(last, out_shape=(jax.ShapeDtypeStruct((32, 8, 8, 128), BF)...  2.01 us

profile of v3, /device:TPU:1, one launch (start us, length us, event | category | flops | bytes accessed | tf_op | source)
XLA Modules:
  0.0 35.2 jit_solution(15486111935985934206)
XLA Ops:
  0.6 32.6 %shard_map.103 = (bf16[32,8,8,128]{3,2,1,0:T(8,128)(2,1)S(1)}, bf16[64,4,4,64]{3,2,1,0:T(4,128)(2,1)S(1)}, bf16[128,8,128]{2,1,0:T(8,128)(2,1)S(1)}, bf16[9,4,64...) custom-call(bf16[32,8,8,128]{3,2,1,0:T(8,128)(2,1)} %feat.1, ...), custom_call_target="tpu_custom_call" | custom-call | tf_op jit(solution)/shard_map/pallas_call | solution.py:451
  33.2 2.0 %shard_map.104 = (bf16[32,8,8,128]{3,2,1,0:T(8,128)(2,1)}, bf16[64,4,4,64]{3,2,1,0:T(4,128)(2,1)}, bf16[512,2,128]{2,1,0:T(2,128)(2,1)}) custom-call(bf16[32,8,8,128]{3,2,1,0:T(8,128)(2,1)S(1)} %get-tuple-element.12.out2_in, bf16[64,4,4,64]{3,2,1,0:T(4,128)(2,1)S(1)} %get-tuple-element.13.out3_in, bf16[128,8,128]{2,1,0:T(8,128)(2,1)S(1)} %get-tuple-element.14.rb, ...), custom_call_target="tpu_custom_call" | custom-call | tf_op jit(solution)/shard_map/pallas_call | solution.py:501

commit v4 on v3

--- a/solution.py
+++ b/solution.py
@@ -209,8 +209,6 @@
     for copy in second:
         copy.start()
 
-    for dx, dy in around:
-        greet(wide_sem.at[0], dx, dy)
     for x in range(1, 9):
         shift(x)
     for copy in others:
@@ -246,10 +244,6 @@
     column = jnp.sum(jnp.where(row == lane, b2[...], 0.0), axis=1, keepdims=True)
     bias2[...] = jnp.broadcast_to(column, (256, 128))
 
-    pl.semaphore_wait(wide_sem.at[0], 8)
-    for dx, dy in around:
-        greet(wide_sem.at[1], 2 * dx, 2 * dy)
-
     for dx in range(3):
         for dz in range(3):
             k = 3 * dx + dz
@@ -287,10 +281,6 @@
     w4[:, 0, :, 128:256] = jnp.zeros((9, 64, 128), BF)
     turn[...] = table("turn_four", 384, 128)
 
-    pl.semaphore_wait(wide_sem.at[1], 8)
-    for dy in (-4, 4):
-        greet(wide_sem.at[2], 0, dy)
-
     fm[0:768, 0:128] = jnp.zeros((768, 128), BF)
     fm[0:768, 1152:1280] = jnp.zeros((768, 128), BF)
     fm[960:1024, :] = jnp.zeros((64, 1280), BF)
@@ -314,6 +304,8 @@
     a2[3, :, 128:256] += mm(t2[2, :, 0:768], fm[0:768, 1152:1280])
     for copy in second:
         copy.wait()
+    for dx, dy in around:
+        greet(wide_sem.at[0], 2 * dx, 2 * dy)
     for x in range(10):
         v = jnp.concatenate([hr[0, x], hr[1, x]], axis=0).astype(F32)
         lanes = slice(x * 128, x * 128 + 128)
@@ -352,6 +344,9 @@
             copy.start()
         third += copies
     d3[576:640, :] = jnp.zeros((64, 640), BF)
+    pl.semaphore_wait(wide_sem.at[0], 8)
+    for dy in (-4, 4):
+        greet(wide_sem.at[1], 0, dy)
     for copy in third:
         copy.wait()
     tiles = []
@@ -386,7 +381,7 @@
         g = table("gather_four", 256, 128, odd * 256)
         block = block + mm(head[odd * 128 : odd * 128 + 128], g) + mm(tail[odd * 128 : odd * 128 + 128], g)
     sa[...] = block.reshape(16, 8, 128).astype(BF)
-    pl.semaphore_wait(wide_sem.at[2], 2)
+    pl.semaphore_wait(wide_sem.at[1], 2)
     me = gx * 16 + gy
     mine = pltpu.make_async_copy(sa.at[gy], rb.at[me], recva_sem)
     y_at, x_at, z_at, core_at = gx // 4 * 2 + gy // 8, gx % 4, gy // 2 % 4, gy % 2
@@ -487,7 +482,7 @@
             pltpu.VMEM((256, 256), BF),
             pltpu.VMEM((16, 8, 128), BF),
             dma((8,)), dma((8,)), dma((8,)), dma((8,)), dma((10,)), dma((10,)),
-            dma, dma, pltpu.SemaphoreType.REGULAR((3,)),
+            dma, dma, pltpu.SemaphoreType.REGULAR((2,)),
         ],
         compiler_params=pltpu.CompilerParams(
             collective_id=0, has_side_effects=True, vmem_limit_bytes=40 * 1024 * 1024

time: 35.4 us -> 32.2 us (0.910)
  Pallas kernels: 34.6 us -> 31.5 us
    pallas_call x1, Pallas kernels: 32.6 us -> 29.5 us  [shards(): pl.pallas_call(kernel, out_shape=(jax.ShapeDtypeStruct((32, 8, 8, 128), B...]
where the time goes in v4:
time: 32.2 us; the launch traced here: 32.1 us
  Pallas kernels  31.5 us (98%)
  between operations  0.64 us (2%)
    pallas_call x1, Pallas kernels, shards(): pl.pallas_call(kernel, out_shape=(jax.ShapeDtypeStruct((32, 8, 8, 128), B...  29.5 us
    pallas_call x1, Pallas kernels, shards(): pl.pallas_call(last, out_shape=(jax.ShapeDtypeStruct((32, 8, 8, 128), BF)...  2.02 us

profile of v4, /device:TPU:1, one launch (start us, length us, event | category | flops | bytes accessed | tf_op | source)
XLA Modules:
  0.0 32.1 jit_solution(11670646183311733798)
XLA Ops:
  0.6 29.5 %shard_map.103 = (bf16[32,8,8,128]{3,2,1,0:T(8,128)(2,1)S(1)}, bf16[64,4,4,64]{3,2,1,0:T(4,128)(2,1)S(1)}, bf16[128,8,128]{2,1,0:T(8,128)(2,1)S(1)}, bf16[9,4,64...) custom-call(bf16[32,8,8,128]{3,2,1,0:T(8,128)(2,1)} %feat.1, ...), custom_call_target="tpu_custom_call" | custom-call | tf_op jit(solution)/shard_map/pallas_call | solution.py:446
  30.1 2.0 %shard_map.104 = (bf16[32,8,8,128]{3,2,1,0:T(8,128)(2,1)}, bf16[64,4,4,64]{3,2,1,0:T(4,128)(2,1)}, bf16[512,2,128]{2,1,0:T(2,128)(2,1)}) custom-call(bf16[32,8,8,128]{3,2,1,0:T(8,128)(2,1)S(1)} %get-tuple-element.12.out2_in, bf16[64,4,4,64]{3,2,1,0:T(4,128)(2,1)S(1)} %get-tuple-element.13.out3_in, bf16[128,8,128]{2,1,0:T(8,128)(2,1)S(1)} %get-tuple-element.14.rb, ...), custom_call_target="tpu_custom_call" | custom-call | tf_op jit(solution)/shard_map/pallas_call | solution.py:496

commit v5 on v4

--- a/solution.py
+++ b/solution.py
@@ -121,7 +121,7 @@
     feat, w2_in, b2_in, w3_in, b3_in, w4_in, b4_in, tab_in,
     out2, out3, rb, w4, turn, b4,
     fx, fm, hs, hr, w2, w3, b2, b3, tab, wc2, z2, t2, a2, wc3, z3, t3, bias2, bias3,
-    pooled, own3, hs3, hr3, d3, l3, sa,
+    pooled, own3, hs3, hr3, d3, a3, l3, sa,
     load_sem, feat_sem, send_sem, recv_sem, send3_sem, recv3_sem, senda_sem, recva_sem, wide_sem,
 ):
     gx, gy = lax.axis_index("gx"), lax.axis_index("gy")
@@ -161,20 +161,12 @@
     for copy in others:
         copy.start()
 
-    pl.semaphore_wait(barrier, 8)
 
     def remote(src, dst, send, recv, x, y):
         return pltpu.make_async_remote_copy(
             src_ref=src, dst_ref=dst, send_sem=send, recv_sem=recv,
             device_id=(x, y), device_id_type=MESH,
         )
-
-    first = [
-        remote(feat.at[:, 7], fx.at[0], send_sem.at[0], recv_sem.at[0], xp, gy),
-        remote(feat.at[:, 0], fx.at[9], send_sem.at[1], recv_sem.at[1], xm, gy),
-    ]
-    for copy in first:
-        copy.start()
 
     def place(x):
         v = fx[x].astype(F32).reshape(256, 128)
@@ -198,6 +190,13 @@
     for side in range(2):
         for x in range(8):
             hs[side, x] = edges[side * 32 : side * 32 + 32, x * 128 : x * 128 + 128]
+    pl.semaphore_wait(barrier, 8)
+    first = [
+        remote(feat.at[:, 7], fx.at[0], send_sem.at[0], recv_sem.at[0], xp, gy),
+        remote(feat.at[:, 0], fx.at[9], send_sem.at[1], recv_sem.at[1], xm, gy),
+    ]
+    for copy in first:
+        copy.start()
     second = [
         remote(hs.at[1, 7], hr.at[0, 0], send_sem.at[4], recv_sem.at[4], xp, yp),
         remote(hs.at[1, 0], hr.at[0, 9], send_sem.at[5], recv_sem.at[5], xm, yp),
@@ -314,10 +313,16 @@
         fm[896:960, lanes] = pltpu.roll(v, 127, 1).astype(BF)
 
     third = []
+
+    def send3(src, dst, x, y):
+        k = len(third)
+        third.append(remote(src, dst, send3_sem.at[k], recv3_sem.at[k], x, y))
+        third[-1].start()
+
     for q in range(2):
         total = jnp.zeros((256, 128), F32)
         for half in range(2):
-            p = 2 * q + half
+            p = ((3, 0), (1, 2))[q][half]
             acc = a2[p]
             for dx in range(3):
                 lanes = slice((p * 2 + dx) * 128, (p * 2 + dx + 2) * 128)
@@ -327,49 +332,53 @@
                 out2[:, 2 * p + x] = v.reshape(32, 8, 128).astype(BF)
                 total = total + mm(v.astype(BF), table("pool_two", 128, 128, half * 256 + x * 128))
         pooled[...] = total
-        own3[q + 1] = (pooled[pl.ds(0, 128, stride=2), :] + pooled[pl.ds(1, 128, stride=2), :]).astype(BF)
-        far, slot = (xm, 3) if q == 0 else (xp, 0)
-        base = 5 * q
-        picked = mm(table("select_three", 64, 128), own3[q + 1]).astype(BF)
+        mean = (pooled[pl.ds(0, 128, stride=2), :] + pooled[pl.ds(1, 128, stride=2), :]).astype(BF)
+        own3[q + 1] = mean
+        picked = mm(table("select_three", 64, 128), mean).astype(BF)
         hs3[0, q] = picked[0:32]
         hs3[1, q] = picked[32:64]
-        copies = [
-            remote(hs3.at[1, q], hr3.at[0, slot], send3_sem.at[base], recv3_sem.at[base], far, yp),
-            remote(hs3.at[0, q], hr3.at[1, slot], send3_sem.at[base + 1], recv3_sem.at[base + 1], far, ym),
-            remote(own3.at[q + 1], own3.at[slot], send3_sem.at[base + 2], recv3_sem.at[base + 2], far, gy),
-            remote(hs3.at[1, q], hr3.at[0, q + 1], send3_sem.at[base + 3], recv3_sem.at[base + 3], gx, yp),
-            remote(hs3.at[0, q], hr3.at[1, q + 1], send3_sem.at[base + 4], recv3_sem.at[base + 4], gx, ym),
-        ]
-        for copy in copies:
-            copy.start()
-        third += copies
+        if q == 0:
+            for x, slot in ((xm, 3), (xp, 0)):
+                send3(hs3.at[1, 0], hr3.at[0, slot], x, yp)
+                send3(hs3.at[0, 0], hr3.at[1, slot], x, ym)
+                send3(own3.at[1], own3.at[slot], x, gy)
+        send3(hs3.at[1, q], hr3.at[0, q + 1], gx, yp)
+        send3(hs3.at[0, q], hr3.at[1, q + 1], gx, ym)
+
+    left = lax.broadcasted_iota(jnp.int32, (128, 128), 1) < 64
+
+    def three(rows, lanes, v):
+        for dz, u in enumerate((rolled_64(v, True), v, rolled_64(v, False))):
+            start = dz * 128 if rows == 128 else 384 + dz * 64
+            d3[start : start + rows, lanes * 128 : lanes * 128 + 128] = u.astype(BF)
+
+    outer, middle = own3[1].astype(F32), own3[2].astype(F32)
+    outer_turned, middle_turned = pltpu.roll(outer, 64, 1), pltpu.roll(middle, 64, 1)
+    three(128, 0, jnp.where(left, outer_turned, middle_turned))
+    three(128, 1, jnp.where(left, middle_turned, outer_turned))
+    three(128, 3, middle)
+    bias = bias3[...]
+    a3[...] = mm(t3[1, :, 0:384], d3[0:384, 0:256]) + jnp.concatenate([bias, bias], axis=1)
     d3[576:640, :] = jnp.zeros((64, 640), BF)
     pl.semaphore_wait(wide_sem.at[0], 8)
     for dy in (-4, 4):
         greet(wide_sem.at[1], 0, dy)
     for copy in third:
         copy.wait()
-    tiles = []
-    for t in range(4):
-        tiles.append(
-            jnp.concatenate([own3[t], hr3[0, t], hr3[1, t]], axis=0).astype(F32)
-        )
-    turned = [pltpu.roll(v, 64, 1) for v in tiles]
-    lane = lax.broadcasted_iota(jnp.int32, (192, 128), 1)
-    between = [jnp.where(lane < 64, turned[t], turned[t + 1]) for t in range(3)]
-    for slot, v in enumerate([tiles[1], tiles[2]] + between):
-        lanes = slice(slot * 128, slot * 128 + 128)
-        for dz, u in enumerate((rolled_64(v, True), v, rolled_64(v, False))):
-            u = u.astype(BF)
-            d3[dz * 128 : dz * 128 + 128, lanes] = u[0:128]
-            d3[384 + dz * 64 : 448 + dz * 64, lanes] = u[128:192]
-    acc = mm(t3[0], d3[:, 256:512]) + mm(t3[1], d3[:, 0:256]) + mm(t3[2], d3[:, 384:640])
-    for q in range(2):
-        v = leaky(acc[:, q * 128 : q * 128 + 128] + bias3[...])
-        l3[:, q * 128 : q * 128 + 128] = v.astype(BF)
-        out3[:, 2 * q] = v[:, 0:64].reshape(64, 4, 64).astype(BF)
-        out3[:, 2 * q + 1] = v[:, 64:128].reshape(64, 4, 64).astype(BF)
-
+    three(128, 2, jnp.where(left, own3[0].astype(F32), outer))
+    three(128, 4, jnp.where(left, outer, own3[3].astype(F32)))
+    edge = [jnp.concatenate([hr3[0, t], hr3[1, t]], axis=0).astype(F32) for t in range(4)]
+    turned = [pltpu.roll(edge[t], 64, 1) for t in (1, 2)]
+    left = lax.broadcasted_iota(jnp.int32, (64, 128), 1) < 64
+    three(64, 0, jnp.where(left, turned[0], turned[1]))
+    three(64, 1, jnp.where(left, turned[1], turned[0]))
+    three(64, 2, jnp.where(left, edge[0], edge[1]))
+    three(64, 3, edge[2])
+    three(64, 4, jnp.where(left, edge[1], edge[3]))
+    v = leaky(
+        a3[...] + mm(t3[0], d3[:, 256:512]) + mm(t3[1, :, 384:640], d3[384:640, 0:256]) + mm(t3[2], d3[:, 384:640])
+    )
+    l3[...] = v.astype(BF)
     sums = mm_t(table("pick_four", 256, 256), l3[...])
     row = lax.broadcasted_iota(jnp.int32, (256, 256), 0) % 2
     lane = lax.broadcasted_iota(jnp.int32, (256, 256), 1) % 4 // 2
@@ -400,6 +409,8 @@
                 layer = layers[dy, dz] + (core_at + flip) % 2
                 remote(sa.at[layer], rb.at[me], senda_sem, recva_sem, columns[dx, dy], layer).start()
     mine.start()
+    for x in range(4):
+        out3[:, x] = l3[:, x * 64 : x * 64 + 64].astype(F32).reshape(64, 4, 64).astype(BF)
     pltpu.make_async_copy(rb, rb, recva_sem).wait()
     pltpu.make_async_copy(rb.at[0:127], rb.at[0:127], senda_sem).wait()
 
@@ -411,13 +422,17 @@
     ]
     for copy in leaving:
         copy.start()
-    for x in range(8):
-        v = rb[x * 16 : x * 16 + 16].astype(F32).reshape(128, 128).astype(BF)
+    for x in range(0, 8, 2):
+        v = jnp.concatenate(
+            [rb[k * 16 : k * 16 + 16].astype(F32).reshape(128, 128).astype(BF) for k in (x, x + 1)], axis=1
+        )
         moved = mm(turn[...], v).astype(BF)
-        for dy in range(3):
-            for half in range(2):
-                start = (dy * 2 + half) * 64
-                pp[dy, (1 + 2 * x) * 32 : (3 + 2 * x) * 32, half * 128 : half * 128 + 128] = moved[start : start + 64]
+        for k in range(2):
+            rows = slice((1 + 2 * (x + k)) * 32, (3 + 2 * (x + k)) * 32)
+            for dy in range(3):
+                for half in range(2):
+                    start = (dy * 2 + half) * 64
+                    pp[dy, rows, half * 128 : half * 128 + 128] = moved[start : start + 64, k * 128 : k * 128 + 128]
     pp[:, 0:32, :] = pp[:, 512:544, :]
     pp[:, 544:576, :] = pp[:, 32:64, :]
     bias = jnp.concatenate([b4[...], b4[...]], axis=1)
@@ -479,6 +494,7 @@
             pltpu.VMEM((2, 2, 32, 128), BF),
             pltpu.VMEM((2, 4, 32, 128), BF),
             pltpu.VMEM((640, 640), BF),
+            pltpu.VMEM((256, 256), F32),
             pltpu.VMEM((256, 256), BF),
             pltpu.VMEM((16, 8, 128), BF),
             dma((8,)), dma((8,)), dma((8,)), dma((8,)), dma((10,)), dma((10,)),

time: 32.2 us -> 31.3 us (0.972)
  Pallas kernels: 31.5 us -> 30.6 us
    pallas_call x1, Pallas kernels: 29.5 us -> 28.6 us  [shards(): pl.pallas_call(kernel, out_shape=(jax.ShapeDtypeStruct((32, 8, 8, 128), B...]
where the time goes in v5:
time: 31.3 us; the launch traced here: 31.2 us
  Pallas kernels  30.6 us (98%)
  between operations  0.64 us (2%)
    pallas_call x1, Pallas kernels, shards(): pl.pallas_call(kernel, out_shape=(jax.ShapeDtypeStruct((32, 8, 8, 128), B...  28.6 us
    pallas_call x1, Pallas kernels, shards(): pl.pallas_call(last, out_shape=(jax.ShapeDtypeStruct((32, 8, 8, 128), BF)...  2 us

profile of v5, /device:TPU:1, one launch (start us, length us, event | category | flops | bytes accessed | tf_op | source)
XLA Modules:
  0.0 31.2 jit_solution(8650673129731726469)
XLA Ops:
  0.6 28.6 %shard_map.103 = (bf16[32,8,8,128]{3,2,1,0:T(8,128)(2,1)S(1)}, bf16[64,4,4,64]{3,2,1,0:T(4,128)(2,1)S(1)}, bf16[128,8,128]{2,1,0:T(8,128)(2,1)S(1)}, bf16[9,4,64...) custom-call(bf16[32,8,8,128]{3,2,1,0:T(8,128)(2,1)} %feat.1, ...), custom_call_target="tpu_custom_call" | custom-call | tf_op jit(solution)/shard_map/pallas_call | solution.py:461
  29.2 2.0 %shard_map.104 = (bf16[32,8,8,128]{3,2,1,0:T(8,128)(2,1)}, bf16[64,4,4,64]{3,2,1,0:T(4,128)(2,1)}, bf16[512,2,128]{2,1,0:T(2,128)(2,1)}) custom-call(bf16[32,8,8,128]{3,2,1,0:T(8,128)(2,1)S(1)} %get-tuple-element.12.out2_in, bf16[64,4,4,64]{3,2,1,0:T(4,128)(2,1)S(1)} %get-tuple-element.13.out3_in, bf16[128,8,128]{2,1,0:T(8,128)(2,1)S(1)} %get-tuple-element.14.rb, ...), custom_call_target="tpu_custom_call" | custom-call | tf_op jit(solution)/shard_map/pallas_call | solution.py:512

commit v6 on v5

--- a/solution.py
+++ b/solution.py
@@ -158,8 +158,6 @@
     ]
     for copy in loads:
         copy.start()
-    for copy in others:
-        copy.start()
 
 
     def remote(src, dst, send, recv, x, y):
@@ -184,6 +182,8 @@
     select = jnp.where(lane == row % 32 * 8 + row // 32 * 7, 1.0, 0.0).astype(BF)
     for copy in loads:
         copy.wait()
+    for copy in others:
+        copy.start()
     for x in range(1, 9):
         place(x)
     edges = mm(select, fm[256:512, 128:1152]).astype(BF)
@@ -191,12 +191,6 @@
         for x in range(8):
             hs[side, x] = edges[side * 32 : side * 32 + 32, x * 128 : x * 128 + 128]
     pl.semaphore_wait(barrier, 8)
-    first = [
-        remote(feat.at[:, 7], fx.at[0], send_sem.at[0], recv_sem.at[0], xp, gy),
-        remote(feat.at[:, 0], fx.at[9], send_sem.at[1], recv_sem.at[1], xm, gy),
-    ]
-    for copy in first:
-        copy.start()
     second = [
         remote(hs.at[1, 7], hr.at[0, 0], send_sem.at[4], recv_sem.at[4], xp, yp),
         remote(hs.at[1, 0], hr.at[0, 9], send_sem.at[5], recv_sem.at[5], xm, yp),
@@ -205,7 +199,15 @@
         remote(hs.at[1], hr.at[0, 1:9], send_sem.at[2], recv_sem.at[2], gx, yp),
         remote(hs.at[0], hr.at[1, 1:9], send_sem.at[3], recv_sem.at[3], gx, ym),
     ]
-    for copy in second:
+    for copy in second[:4]:
+        copy.start()
+    first = [
+        remote(fx.at[8], fx.at[0], send_sem.at[0], recv_sem.at[0], xp, gy),
+        remote(fx.at[1], fx.at[9], send_sem.at[1], recv_sem.at[1], xm, gy),
+    ]
+    for copy in first:
+        copy.start()
+    for copy in second[4:]:
         copy.start()
 
     for x in range(1, 9):
@@ -242,6 +244,74 @@
     lane = lax.broadcasted_iota(jnp.int32, (256, 32), 1)
     column = jnp.sum(jnp.where(row == lane, b2[...], 0.0), axis=1, keepdims=True)
     bias2[...] = jnp.broadcast_to(column, (256, 128))
+
+    fm[0:768, 0:128] = jnp.zeros((768, 128), BF)
+    fm[0:768, 1152:1280] = jnp.zeros((768, 128), BF)
+    fm[960:1024, :] = jnp.zeros((64, 1280), BF)
+
+    def inner(p, carry):
+        a2[p] = mm(
+            jnp.concatenate([t2[dx, :, 0:768] for dx in range(3)], axis=1),
+            jnp.concatenate(
+                [fm[0:768, pl.ds(pl.multiple_of((p * 2 + dx) * 128, 128), 256)] for dx in range(3)], axis=0
+            ),
+        )
+        return carry
+
+    lax.fori_loop(0, 4, inner, 0)
+
+    for copy in first:
+        copy.wait()
+    for x in (0, 9):
+        place(x)
+        shift(x)
+    a2[0, :, 0:128] += mm(t2[0, :, 0:768], fm[0:768, 0:128])
+    a2[3, :, 128:256] += mm(t2[2, :, 0:768], fm[0:768, 1152:1280])
+    for copy in second:
+        copy.wait()
+    for dx, dy in around:
+        greet(wide_sem.at[0], 2 * dx, 2 * dy)
+    for x in range(10):
+        v = jnp.concatenate([hr[0, x], hr[1, x]], axis=0).astype(F32)
+        lanes = slice(x * 128, x * 128 + 128)
+        fm[768:832, lanes] = pltpu.roll(v, 1, 1).astype(BF)
+        fm[832:896, lanes] = v.astype(BF)
+        fm[896:960, lanes] = pltpu.roll(v, 127, 1).astype(BF)
+
+    third = []
+
+    def send3(src, dst, x, y):
+        k = len(third)
+        third.append(remote(src, dst, send3_sem.at[k], recv3_sem.at[k], x, y))
+        third[-1].start()
+
+    for q in range(2):
+        total = jnp.zeros((256, 128), F32)
+        for half in range(2):
+            p = ((3, 0), (1, 2))[q][half]
+            acc = a2[p] + mm(
+                jnp.concatenate([t2[dx, :, 768:1024] for dx in range(3)], axis=1),
+                jnp.concatenate(
+                    [fm[768:1024, (p * 2 + dx) * 128 : (p * 2 + dx + 2) * 128] for dx in range(3)], axis=0
+                ),
+            )
+            for x in range(2):
+                v = leaky(acc[:, x * 128 : x * 128 + 128] + bias2[...])
+                out2[:, 2 * p + x] = v.reshape(32, 8, 128).astype(BF)
+                total = total + mm(v.astype(BF), table("pool_two", 128, 128, half * 256 + x * 128))
+        pooled[...] = total
+        mean = (pooled[pl.ds(0, 128, stride=2), :] + pooled[pl.ds(1, 128, stride=2), :]).astype(BF)
+        own3[q + 1] = mean
+        picked = mm(table("select_three", 64, 128), mean).astype(BF)
+        hs3[0, q] = picked[0:32]
+        hs3[1, q] = picked[32:64]
+        if q == 0:
+            for x, slot in ((xm, 3), (xp, 0)):
+                send3(hs3.at[1, 0], hr3.at[0, slot], x, yp)
+                send3(hs3.at[0, 0], hr3.at[1, slot], x, ym)
+                send3(own3.at[1], own3.at[slot], x, gy)
+        send3(hs3.at[1, q], hr3.at[0, q + 1], gx, yp)
+        send3(hs3.at[0, q], hr3.at[1, q + 1], gx, ym)
 
     for dx in range(3):
         for dz in range(3):
@@ -279,71 +349,6 @@
     w4[:, 3, :, 0:128] = jnp.zeros((9, 64, 128), BF)
     w4[:, 0, :, 128:256] = jnp.zeros((9, 64, 128), BF)
     turn[...] = table("turn_four", 384, 128)
-
-    fm[0:768, 0:128] = jnp.zeros((768, 128), BF)
-    fm[0:768, 1152:1280] = jnp.zeros((768, 128), BF)
-    fm[960:1024, :] = jnp.zeros((64, 1280), BF)
-
-    def inner(p, carry):
-        acc = jnp.zeros((256, 256), F32)
-        for dx in range(3):
-            lanes = pl.ds(pl.multiple_of((p * 2 + dx) * 128, 128), 256)
-            acc = acc + mm(t2[dx, :, 0:768], fm[0:768, lanes])
-        a2[p] = acc
-        return carry
-
-    lax.fori_loop(0, 4, inner, 0)
-
-    for copy in first:
-        copy.wait()
-    for x in (0, 9):
-        place(x)
-        shift(x)
-    a2[0, :, 0:128] += mm(t2[0, :, 0:768], fm[0:768, 0:128])
-    a2[3, :, 128:256] += mm(t2[2, :, 0:768], fm[0:768, 1152:1280])
-    for copy in second:
-        copy.wait()
-    for dx, dy in around:
-        greet(wide_sem.at[0], 2 * dx, 2 * dy)
-    for x in range(10):
-        v = jnp.concatenate([hr[0, x], hr[1, x]], axis=0).astype(F32)
-        lanes = slice(x * 128, x * 128 + 128)
-        fm[768:832, lanes] = pltpu.roll(v, 1, 1).astype(BF)
-        fm[832:896, lanes] = v.astype(BF)
-        fm[896:960, lanes] = pltpu.roll(v, 127, 1).astype(BF)
-
-    third = []
-
-    def send3(src, dst, x, y):
-        k = len(third)
-        third.append(remote(src, dst, send3_sem.at[k], recv3_sem.at[k], x, y))
-        third[-1].start()
-
-    for q in range(2):
-        total = jnp.zeros((256, 128), F32)
-        for half in range(2):
-            p = ((3, 0), (1, 2))[q][half]
-            acc = a2[p]
-            for dx in range(3):
-                lanes = slice((p * 2 + dx) * 128, (p * 2 + dx + 2) * 128)
-                acc = acc + mm(t2[dx, :, 768:1024], fm[768:1024, lanes])
-            for x in range(2):
-                v = leaky(acc[:, x * 128 : x * 128 + 128] + bias2[...])
-                out2[:, 2 * p + x] = v.reshape(32, 8, 128).astype(BF)
-                total = total + mm(v.astype(BF), table("pool_two", 128, 128, half * 256 + x * 128))
-        pooled[...] = total
-        mean = (pooled[pl.ds(0, 128, stride=2), :] + pooled[pl.ds(1, 128, stride=2), :]).astype(BF)
-        own3[q + 1] = mean
-        picked = mm(table("select_three", 64, 128), mean).astype(BF)
-        hs3[0, q] = picked[0:32]
-        hs3[1, q] = picked[32:64]
-        if q == 0:
-            for x, slot in ((xm, 3), (xp, 0)):
-                send3(hs3.at[1, 0], hr3.at[0, slot], x, yp)
-                send3(hs3.at[0, 0], hr3.at[1, slot], x, ym)
-                send3(own3.at[1], own3.at[slot], x, gy)
-        send3(hs3.at[1, q], hr3.at[0, q + 1], gx, yp)
-        send3(hs3.at[0, q], hr3.at[1, q + 1], gx, ym)
 
     left = lax.broadcasted_iota(jnp.int32, (128, 128), 1) < 64
 
@@ -437,12 +442,8 @@
     pp[:, 544:576, :] = pp[:, 32:64, :]
     bias = jnp.concatenate([b4[...], b4[...]], axis=1)
     for m in range(2):
-        acc = jnp.zeros((256, 256), F32)
-        for dx in range(3):
-            for dy in range(3):
-                rows = slice(m * 256 + dx * 32, m * 256 + dx * 32 + 256)
-                acc = acc + mm(pp[dy, rows, :], w4[3 * dx + dy].reshape(256, 256))
-        v = leaky(acc + bias)
+        rows = [pp[dy, m * 256 + dx * 32 : m * 256 + dx * 32 + 256, :] for dx in range(3) for dy in range(3)]
+        v = leaky(mm(jnp.concatenate(rows, axis=1), w4[...].reshape(2304, 256)) + bias)
         l4[m * 256 : m * 256 + 256] = v.reshape(256, 2, 128).astype(BF)
         piece = pl.ds(m * 256, 256)
         leaving.append(pltpu.make_async_copy(l4.at[piece], out4.at[piece], sem.at[2 + m]))

time: 31.3 us -> 31.1 us (level)
  no operation moved by 1% of the time
where the time goes in v6:
time: 31.1 us; the launch traced here: 30.9 us
  Pallas kernels  30.3 us (97%)
  between operations  0.64 us (2%)
    pallas_call x1, Pallas kernels, shards(): pl.pallas_call(kernel, out_shape=(jax.ShapeDtypeStruct((32, 8, 8, 128), B...  28.3 us
    pallas_call x1, Pallas kernels, shards(): pl.pallas_call(last, out_shape=(jax.ShapeDtypeStruct((32, 8, 8, 128), BF)...  1.97 us

profile of v6, /device:TPU:1, one launch (start us, length us, event | category | flops | bytes accessed | tf_op | source)
XLA Modules:
  0.0 30.9 jit_solution(10579697625058916836)
XLA Ops:
  0.6 28.3 %shard_map.103 = (bf16[32,8,8,128]{3,2,1,0:T(8,128)(2,1)S(1)}, bf16[64,4,4,64]{3,2,1,0:T(4,128)(2,1)S(1)}, bf16[128,8,128]{2,1,0:T(8,128)(2,1)S(1)}, bf16[9,4,64...) custom-call(bf16[32,8,8,128]{3,2,1,0:T(8,128)(2,1)} %feat.1, ...), custom_call_target="tpu_custom_call" | custom-call | tf_op jit(solution)/shard_map/pallas_call | solution.py:462
  28.9 2.0 %shard_map.104 = (bf16[32,8,8,128]{3,2,1,0:T(8,128)(2,1)}, bf16[64,4,4,64]{3,2,1,0:T(4,128)(2,1)}, bf16[512,2,128]{2,1,0:T(2,128)(2,1)}) custom-call(bf16[32,8,8,128]{3,2,1,0:T(8,128)(2,1)S(1)} %get-tuple-element.12.out2_in, bf16[64,4,4,64]{3,2,1,0:T(4,128)(2,1)S(1)} %get-tuple-element.13.out3_in, bf16[128,8,128]{2,1,0:T(8,128)(2,1)S(1)} %get-tuple-element.14.rb, ...), custom_call_target="tpu_custom_call" | custom-call | tf_op jit(solution)/shard_map/pallas_call | solution.py:513

commit v7 on v6

--- a/solution.py
+++ b/solution.py
@@ -11,6 +11,7 @@
 BF = jnp.bfloat16
 F32 = jnp.float32
 MESH = pl.DeviceIdType.MESH
+PIECES = 2
 
 
 def tables():
@@ -119,9 +120,9 @@
 
 def kernel(
     feat, w2_in, b2_in, w3_in, b3_in, w4_in, b4_in, tab_in,
-    out2, out3, rb, w4, turn, b4,
+    out2, out3, pp, w4, b4,
     fx, fm, hs, hr, w2, w3, b2, b3, tab, wc2, z2, t2, a2, wc3, z3, t3, bias2, bias3,
-    pooled, own3, hs3, hr3, d3, a3, l3, sa,
+    pooled, own3, hs3, hr3, d3, a3, l3, sa, rb,
     load_sem, feat_sem, send_sem, recv_sem, send3_sem, recv3_sem, senda_sem, recva_sem, wide_sem,
 ):
     gx, gy = lax.axis_index("gx"), lax.axis_index("gy")
@@ -156,8 +157,8 @@
         pltpu.make_async_copy(w4_in, w4.at[:, 0:3, :, 0:128], load_sem.at[6]),
         pltpu.make_async_copy(w4_in, w4.at[:, 1:4, :, 128:256], load_sem.at[7]),
     ]
-    for copy in loads:
-        copy.start()
+    for x in (0, 7, 1, 2, 3, 4, 5, 6):
+        loads[x].start()
 
 
     def remote(src, dst, send, recv, x, y):
@@ -180,17 +181,19 @@
     row = lax.broadcasted_iota(jnp.int32, (64, 256), 0)
     lane = lax.broadcasted_iota(jnp.int32, (64, 256), 1)
     select = jnp.where(lane == row % 32 * 8 + row // 32 * 7, 1.0, 0.0).astype(BF)
-    for copy in loads:
-        copy.wait()
-    for copy in others:
-        copy.start()
-    for x in range(1, 9):
-        place(x)
-    edges = mm(select, fm[256:512, 128:1152]).astype(BF)
-    for side in range(2):
-        for x in range(8):
-            hs[side, x] = edges[side * 32 : side * 32 + 32, x * 128 : x * 128 + 128]
+    def cut(side_rows, x):
+        for side in range(2):
+            hs[side, x] = side_rows[side * 32 : side * 32 + 32]
+
+    for x in (0, 7):
+        loads[x].wait()
+        place(x + 1)
+        cut(mm(select, fm[256:512, x * 128 + 128 : x * 128 + 256]).astype(BF), x)
     pl.semaphore_wait(barrier, 8)
+    first = [
+        remote(fx.at[8], fx.at[0], send_sem.at[0], recv_sem.at[0], xp, gy),
+        remote(fx.at[1], fx.at[9], send_sem.at[1], recv_sem.at[1], xm, gy),
+    ]
     second = [
         remote(hs.at[1, 7], hr.at[0, 0], send_sem.at[4], recv_sem.at[4], xp, yp),
         remote(hs.at[1, 0], hr.at[0, 9], send_sem.at[5], recv_sem.at[5], xm, yp),
@@ -199,14 +202,16 @@
         remote(hs.at[1], hr.at[0, 1:9], send_sem.at[2], recv_sem.at[2], gx, yp),
         remote(hs.at[0], hr.at[1, 1:9], send_sem.at[3], recv_sem.at[3], gx, ym),
     ]
-    for copy in second[:4]:
+    for copy in second[:4] + first:
         copy.start()
-    first = [
-        remote(fx.at[8], fx.at[0], send_sem.at[0], recv_sem.at[0], xp, gy),
-        remote(fx.at[1], fx.at[9], send_sem.at[1], recv_sem.at[1], xm, gy),
-    ]
-    for copy in first:
+    for x in range(1, 7):
+        loads[x].wait()
+        place(x + 1)
+    for copy in others:
         copy.start()
+    edges = mm(select, fm[256:512, 256:1024]).astype(BF)
+    for x in range(1, 7):
+        cut(edges[:, (x - 1) * 128 : x * 128], x)
     for copy in second[4:]:
         copy.start()
 
@@ -348,7 +353,6 @@
 
     w4[:, 3, :, 0:128] = jnp.zeros((9, 64, 128), BF)
     w4[:, 0, :, 128:256] = jnp.zeros((9, 64, 128), BF)
-    turn[...] = table("turn_four", 384, 128)
 
     left = lax.broadcasted_iota(jnp.int32, (128, 128), 1) < 64
 
@@ -397,7 +401,7 @@
     sa[...] = block.reshape(16, 8, 128).astype(BF)
     pl.semaphore_wait(wide_sem.at[1], 2)
     me = gx * 16 + gy
-    mine = pltpu.make_async_copy(sa.at[gy], rb.at[me], recva_sem)
+    mine = pltpu.make_async_copy(sa.at[gy], rb.at[me], recva_sem.at[gx])
     y_at, x_at, z_at, core_at = gx // 4 * 2 + gy // 8, gx % 4, gy // 2 % 4, gy % 2
     columns, layers = {}, {}
     for d in range(4):
@@ -412,40 +416,47 @@
         for flip in range(2):
             if dx or dy or dz or flip:
                 layer = layers[dy, dz] + (core_at + flip) % 2
-                remote(sa.at[layer], rb.at[me], senda_sem, recva_sem, columns[dx, dy], layer).start()
+                remote(sa.at[layer], rb.at[me], senda_sem, recva_sem.at[gx], columns[dx, dy], layer).start()
     mine.start()
     for x in range(4):
         out3[:, x] = l3[:, x * 64 : x * 64 + 64].astype(F32).reshape(64, 4, 64).astype(BF)
-    pltpu.make_async_copy(rb, rb, recva_sem).wait()
+    for dy in (0, 2):
+        for dx in (0, 1, 3, 2):
+            g = columns[dx, dy]
+            here = pl.ds(g * 16, 16)
+            pltpu.make_async_copy(rb.at[here], rb.at[here], recva_sem.at[g]).wait()
+            moved = mm(table("turn_four", 384, 128), rb[here].astype(F32).reshape(128, 128).astype(BF)).astype(BF)
+            rows = pl.ds(pl.multiple_of(g * 64, 64), 64)
+            for k in range(6):
+                lanes = slice(k % 2 * 128, k % 2 * 128 + 128)
+                pp[k // 2, rows, lanes] = moved[k * 64 : k * 64 + 64]
     pltpu.make_async_copy(rb.at[0:127], rb.at[0:127], senda_sem).wait()
 
 
-def last(out2_in, out3_in, rb, w4, turn, b4, out2, out3, out4, pp, l4, sem):
+def last(out2_in, out3_in, pp, w4, b4, out2, out3, out4, l4, sem):
     leaving = [
         pltpu.make_async_copy(out2_in, out2, sem.at[0]),
         pltpu.make_async_copy(out3_in, out3, sem.at[1]),
     ]
     for copy in leaving:
         copy.start()
-    for x in range(0, 8, 2):
-        v = jnp.concatenate(
-            [rb[k * 16 : k * 16 + 16].astype(F32).reshape(128, 128).astype(BF) for k in (x, x + 1)], axis=1
-        )
-        moved = mm(turn[...], v).astype(BF)
-        for k in range(2):
-            rows = slice((1 + 2 * (x + k)) * 32, (3 + 2 * (x + k)) * 32)
+    bias = jnp.concatenate([b4[...], b4[...]], axis=1)
+    size = 512 // PIECES
+    for m in range(PIECES):
+        operands = []
+        for dx in range(3):
+            start = m * size + (dx - 1) * 32
             for dy in range(3):
-                for half in range(2):
-                    start = (dy * 2 + half) * 64
-                    pp[dy, rows, half * 128 : half * 128 + 128] = moved[start : start + 64, k * 128 : k * 128 + 128]
-    pp[:, 0:32, :] = pp[:, 512:544, :]
-    pp[:, 544:576, :] = pp[:, 32:64, :]
-    bias = jnp.concatenate([b4[...], b4[...]], axis=1)
-    for m in range(2):
-        rows = [pp[dy, m * 256 + dx * 32 : m * 256 + dx * 32 + 256, :] for dx in range(3) for dy in range(3)]
-        v = leaky(mm(jnp.concatenate(rows, axis=1), w4[...].reshape(2304, 256)) + bias)
-        l4[m * 256 : m * 256 + 256] = v.reshape(256, 2, 128).astype(BF)
-        piece = pl.ds(m * 256, 256)
+                if start < 0:
+                    v = jnp.concatenate([pp[dy, 480:512, :], pp[dy, 0 : size - 32, :]], axis=0)
+                elif start + size > 512:
+                    v = jnp.concatenate([pp[dy, start:512, :], pp[dy, 0:32, :]], axis=0)
+                else:
+                    v = pp[dy, start : start + size, :]
+                operands.append(v)
+        v = leaky(mm(jnp.concatenate(operands, axis=1), w4[...].reshape(2304, 256)) + bias)
+        piece = slice(m * size, m * size + size)
+        l4[piece] = v.reshape(size, 2, 128).astype(BF)
         leaving.append(pltpu.make_async_copy(l4.at[piece], out4.at[piece], sem.at[2 + m]))
         leaving[-1].start()
     for copy in leaving:
@@ -464,13 +475,12 @@
         out_shape=(
             jax.ShapeDtypeStruct((32, 8, 8, 128), BF),
             jax.ShapeDtypeStruct((64, 4, 4, 64), BF),
-            jax.ShapeDtypeStruct((128, 8, 128), BF),
+            jax.ShapeDtypeStruct((3, 512, 256), BF),
             jax.ShapeDtypeStruct((9, 4, 64, 256), BF),
-            jax.ShapeDtypeStruct((384, 128), BF),
             jax.ShapeDtypeStruct((1, 128), F32),
         ),
         in_specs=[hbm] * 8,
-        out_specs=(vm,) * 6,
+        out_specs=(vm,) * 5,
         scratch_shapes=[
             pltpu.VMEM((10, 32, 8, 128), BF),
             pltpu.VMEM((1024, 1280), BF),
@@ -498,8 +508,9 @@
             pltpu.VMEM((256, 256), F32),
             pltpu.VMEM((256, 256), BF),
             pltpu.VMEM((16, 8, 128), BF),
+            pltpu.VMEM((128, 8, 128), BF),
             dma((8,)), dma((8,)), dma((8,)), dma((8,)), dma((10,)), dma((10,)),
-            dma, dma, pltpu.SemaphoreType.REGULAR((2,)),
+            dma, dma((8,)), pltpu.SemaphoreType.REGULAR((2,)),
         ],
         compiler_params=pltpu.CompilerParams(
             collective_id=0, has_side_effects=True, vmem_limit_bytes=40 * 1024 * 1024
@@ -517,12 +528,11 @@
             jax.ShapeDtypeStruct((64, 4, 4, 64), BF),
             jax.ShapeDtypeStruct((512, 2, 128), BF),
         ),
-        in_specs=[vm] * 6,
+        in_specs=[vm] * 5,
         out_specs=(hbm,) * 3,
         scratch_shapes=[
-            pltpu.VMEM((3, 576, 256), BF),
             pltpu.VMEM((512, 2, 128), BF),
-            dma((4,)),
+            dma((2 + PIECES,)),
         ],
         compiler_params=pltpu.CompilerParams(vmem_limit_bytes=40 * 1024 * 1024),
     )(*held)

time: 31.1 us -> 32.1 us (1.032)
  Pallas kernels: 30.3 us -> 31.3 us
    pallas_call x1, Pallas kernels: 28.3 us -> 29.6 us  [shards(): pl.pallas_call(kernel, out_shape=(jax.ShapeDtypeStruct((32, 8, 8, 128), B...]
where the time goes in v7:
time: 32.1 us; the launch traced here: 32 us
  Pallas kernels  31.3 us (98%)
  between operations  0.64 us (2%)
    pallas_call x1, Pallas kernels, shards(): pl.pallas_call(kernel, out_shape=(jax.ShapeDtypeStruct((32, 8, 8, 128), B...  29.6 us
    pallas_call x1, Pallas kernels, shards(): pl.pallas_call(last, out_shape=(jax.ShapeDtypeStruct((32, 8, 8, 128), BF)...  1.72 us

profile of v7, /device:TPU:1, one launch (start us, length us, event | category | flops | bytes accessed | tf_op | source)
XLA Modules:
  0.0 32.0 jit_solution(1383368328452995850)
XLA Ops:
  0.6 29.6 %shard_map.103 = (bf16[32,8,8,128]{3,2,1,0:T(8,128)(2,1)S(1)}, bf16[64,4,4,64]{3,2,1,0:T(4,128)(2,1)S(1)}, bf16[3,512,256]{2,1,0:T(8,128)(2,1)S(1)}, bf16[9,4,64,256]{3,2,1,0:T(8,128)(2,1)S(1)}, f32[1,128]{1,0:T(1,128)S(1)}) custom-call(bf16[32,8,8,128]{3,2,1,0:T(8,128)(2,1)} %feat.1, bf16[27,32,32]{2,1,0:T(8,128)(2,1)} %w2_in.1, f32[1,32]{1,0:T(1,128)} %bitcast.12, ...), custom_call_target="tpu_custom_call" | custom-call | tf_op jit(solution)/shard_map/pallas_call | solution.py:473
  30.2 1.7 %shard_map.104 = (bf16[32,8,8,128]{3,2,1,0:T(8,128)(2,1)}, bf16[64,4,4,64]{3,2,1,0:T(4,128)(2,1)}, bf16[512,2,128]{2,1,0:T(2,128)(2,1)}) custom-call(bf16[32,8,8,128]{3,2,1,0:T(8,128)(2,1)S(1)} %get-tuple-element.11.out2_in, bf16[64,4,4,64]{3,2,1,0:T(4,128)(2,1)S(1)} %get-tuple-element.12.out3_in, bf16[3,512,256]{2,1,0:T(8,128)(2,1)S(1)} %get-tuple-element.13.pp, ...), custom_call_target="tpu_custom_call" | custom-call | tf_op jit(solution)/shard_map/pallas_call | solution.py:524

commit v8 on v7

--- a/solution.py
+++ b/solution.py
@@ -120,9 +120,9 @@
 
 def kernel(
     feat, w2_in, b2_in, w3_in, b3_in, w4_in, b4_in, tab_in,
-    out2, out3, pp, w4, b4,
+    out2, out3, rb, w4, turn, b4,
     fx, fm, hs, hr, w2, w3, b2, b3, tab, wc2, z2, t2, a2, wc3, z3, t3, bias2, bias3,
-    pooled, own3, hs3, hr3, d3, a3, l3, sa, rb,
+    pooled, own3, hs3, hr3, d3, a3, l3, sa,
     load_sem, feat_sem, send_sem, recv_sem, send3_sem, recv3_sem, senda_sem, recva_sem, wide_sem,
 ):
     gx, gy = lax.axis_index("gx"), lax.axis_index("gy")
@@ -159,6 +159,8 @@
     ]
     for x in (0, 7, 1, 2, 3, 4, 5, 6):
         loads[x].start()
+    for copy in others:
+        copy.start()
 
 
     def remote(src, dst, send, recv, x, y):
@@ -207,8 +209,6 @@
     for x in range(1, 7):
         loads[x].wait()
         place(x + 1)
-    for copy in others:
-        copy.start()
     edges = mm(select, fm[256:512, 256:1024]).astype(BF)
     for x in range(1, 7):
         cut(edges[:, (x - 1) * 128 : x * 128], x)
@@ -401,7 +401,7 @@
     sa[...] = block.reshape(16, 8, 128).astype(BF)
     pl.semaphore_wait(wide_sem.at[1], 2)
     me = gx * 16 + gy
-    mine = pltpu.make_async_copy(sa.at[gy], rb.at[me], recva_sem.at[gx])
+    mine = pltpu.make_async_copy(sa.at[gy], rb.at[me], recva_sem)
     y_at, x_at, z_at, core_at = gx // 4 * 2 + gy // 8, gx % 4, gy // 2 % 4, gy % 2
     columns, layers = {}, {}
     for d in range(4):
@@ -416,30 +416,33 @@
         for flip in range(2):
             if dx or dy or dz or flip:
                 layer = layers[dy, dz] + (core_at + flip) % 2
-                remote(sa.at[layer], rb.at[me], senda_sem, recva_sem.at[gx], columns[dx, dy], layer).start()
+                remote(sa.at[layer], rb.at[me], senda_sem, recva_sem, columns[dx, dy], layer).start()
     mine.start()
     for x in range(4):
         out3[:, x] = l3[:, x * 64 : x * 64 + 64].astype(F32).reshape(64, 4, 64).astype(BF)
-    for dy in (0, 2):
-        for dx in (0, 1, 3, 2):
-            g = columns[dx, dy]
-            here = pl.ds(g * 16, 16)
-            pltpu.make_async_copy(rb.at[here], rb.at[here], recva_sem.at[g]).wait()
-            moved = mm(table("turn_four", 384, 128), rb[here].astype(F32).reshape(128, 128).astype(BF)).astype(BF)
-            rows = pl.ds(pl.multiple_of(g * 64, 64), 64)
-            for k in range(6):
-                lanes = slice(k % 2 * 128, k % 2 * 128 + 128)
-                pp[k // 2, rows, lanes] = moved[k * 64 : k * 64 + 64]
+    turn[...] = table("turn_four", 384, 128)
+    pltpu.make_async_copy(rb, rb, recva_sem).wait()
     pltpu.make_async_copy(rb.at[0:127], rb.at[0:127], senda_sem).wait()
 
 
-def last(out2_in, out3_in, pp, w4, b4, out2, out3, out4, l4, sem):
+def last(out2_in, out3_in, rb, w4, turn, b4, out2, out3, out4, pp, l4, sem):
     leaving = [
         pltpu.make_async_copy(out2_in, out2, sem.at[0]),
         pltpu.make_async_copy(out3_in, out3, sem.at[1]),
     ]
     for copy in leaving:
         copy.start()
+    for x in range(0, 8, 2):
+        v = jnp.concatenate(
+            [rb[k * 16 : k * 16 + 16].astype(F32).reshape(128, 128).astype(BF) for k in (x, x + 1)], axis=1
+        )
+        moved = mm(turn[...], v).astype(BF)
+        for k in range(2):
+            rows = slice((x + k) * 64, (x + k) * 64 + 64)
+            for dy in range(3):
+                for half in range(2):
+                    start = (dy * 2 + half) * 64
+                    pp[dy, rows, half * 128 : half * 128 + 128] = moved[start : start + 64, k * 128 : k * 128 + 128]
     bias = jnp.concatenate([b4[...], b4[...]], axis=1)
     size = 512 // PIECES
     for m in range(PIECES):
@@ -475,12 +478,13 @@
         out_shape=(
             jax.ShapeDtypeStruct((32, 8, 8, 128), BF),
             jax.ShapeDtypeStruct((64, 4, 4, 64), BF),
-            jax.ShapeDtypeStruct((3, 512, 256), BF),
+            jax.ShapeDtypeStruct((128, 8, 128), BF),
             jax.ShapeDtypeStruct((9, 4, 64, 256), BF),
+            jax.ShapeDtypeStruct((384, 128), BF),
             jax.ShapeDtypeStruct((1, 128), F32),
         ),
         in_specs=[hbm] * 8,
-        out_specs=(vm,) * 5,
+        out_specs=(vm,) * 6,
         scratch_shapes=[
             pltpu.VMEM((10, 32, 8, 128), BF),
             pltpu.VMEM((1024, 1280), BF),
@@ -508,9 +512,8 @@
             pltpu.VMEM((256, 256), F32),
             pltpu.VMEM((256, 256), BF),
             pltpu.VMEM((16, 8, 128), BF),
-            pltpu.VMEM((128, 8, 128), BF),
             dma((8,)), dma((8,)), dma((8,)), dma((8,)), dma((10,)), dma((10,)),
-            dma, dma((8,)), pltpu.SemaphoreType.REGULAR((2,)),
+            dma, dma, pltpu.SemaphoreType.REGULAR((2,)),
         ],
         compiler_params=pltpu.CompilerParams(
             collective_id=0, has_side_effects=True, vmem_limit_bytes=40 * 1024 * 1024
@@ -528,9 +531,10 @@
             jax.ShapeDtypeStruct((64, 4, 4, 64), BF),
             jax.ShapeDtypeStruct((512, 2, 128), BF),
         ),
-        in_specs=[vm] * 5,
+        in_specs=[vm] * 6,
         out_specs=(hbm,) * 3,
         scratch_shapes=[
+            pltpu.VMEM((3, 512, 256), BF),
             pltpu.VMEM((512, 2, 128), BF),
             dma((2 + PIECES,)),
         ],

time: 32.1 us -> 30.9 us (0.963)
  Pallas kernels: 31.3 us -> 30.2 us
    pallas_call x1, Pallas kernels: 29.6 us -> 28.2 us  [shards(): pl.pallas_call(kernel, out_shape=(jax.ShapeDtypeStruct((32, 8, 8, 128), B...]
where the time goes in v8:
time: 30.9 us; the launch traced here: 30.8 us
  Pallas kernels  30.2 us (98%)
  between operations  0.64 us (2%)
    pallas_call x1, Pallas kernels, shards(): pl.pallas_call(kernel, out_shape=(jax.ShapeDtypeStruct((32, 8, 8, 128), B...  28.2 us
    pallas_call x1, Pallas kernels, shards(): pl.pallas_call(last, out_shape=(jax.ShapeDtypeStruct((32, 8, 8, 128), BF)...  1.97 us

profile of v8, /device:TPU:1, one launch (start us, length us, event | category | flops | bytes accessed | tf_op | source)
XLA Modules:
  0.0 30.8 jit_solution(15662890782174224690)
XLA Ops:
  0.6 28.2 %shard_map.103 = (bf16[32,8,8,128]{3,2,1,0:T(8,128)(2,1)S(1)}, bf16[64,4,4,64]{3,2,1,0:T(4,128)(2,1)S(1)}, bf16[128,8,128]{2,1,0:T(8,128)(2,1)S(1)}, bf16[9,4,64...) custom-call(bf16[32,8,8,128]{3,2,1,0:T(8,128)(2,1)} %feat.1, ...), custom_call_target="tpu_custom_call" | custom-call | tf_op jit(solution)/shard_map/pallas_call | solution.py:476
  28.8 2.0 %shard_map.104 = (bf16[32,8,8,128]{3,2,1,0:T(8,128)(2,1)}, bf16[64,4,4,64]{3,2,1,0:T(4,128)(2,1)}, bf16[512,2,128]{2,1,0:T(2,128)(2,1)}) custom-call(bf16[32,8,8,128]{3,2,1,0:T(8,128)(2,1)S(1)} %get-tuple-element.12.out2_in, bf16[64,4,4,64]{3,2,1,0:T(4,128)(2,1)S(1)} %get-tuple-element.13.out3_in, bf16[128,8,128]{2,1,0:T(8,128)(2,1)S(1)} %get-tuple-element.14.rb, ...), custom_call_target="tpu_custom_call" | custom-call | tf_op jit(solution)/shard_map/pallas_call | solution.py:527

commit v9 on v8

--- a/solution.py
+++ b/solution.py
@@ -122,7 +122,7 @@
     feat, w2_in, b2_in, w3_in, b3_in, w4_in, b4_in, tab_in,
     out2, out3, rb, w4, turn, b4,
     fx, fm, hs, hr, w2, w3, b2, b3, tab, wc2, z2, t2, a2, wc3, z3, t3, bias2, bias3,
-    pooled, own3, hs3, hr3, d3, a3, l3, sa,
+    pooled, l2, own3, hs3, hr3, d3, a3, l3, sa,
     load_sem, feat_sem, send_sem, recv_sem, send3_sem, recv3_sem, senda_sem, recva_sem, wide_sem,
 ):
     gx, gy = lax.axis_index("gx"), lax.axis_index("gy")
@@ -265,18 +265,7 @@
 
     lax.fori_loop(0, 4, inner, 0)
 
-    for copy in first:
-        copy.wait()
-    for x in (0, 9):
-        place(x)
-        shift(x)
-    a2[0, :, 0:128] += mm(t2[0, :, 0:768], fm[0:768, 0:128])
-    a2[3, :, 128:256] += mm(t2[2, :, 0:768], fm[0:768, 1152:1280])
-    for copy in second:
-        copy.wait()
-    for dx, dy in around:
-        greet(wide_sem.at[0], 2 * dx, 2 * dy)
-    for x in range(10):
+    def edge_rows(x):
         v = jnp.concatenate([hr[0, x], hr[1, x]], axis=0).astype(F32)
         lanes = slice(x * 128, x * 128 + 128)
         fm[768:832, lanes] = pltpu.roll(v, 1, 1).astype(BF)
@@ -290,7 +279,7 @@
         third.append(remote(src, dst, send3_sem.at[k], recv3_sem.at[k], x, y))
         third[-1].start()
 
-    for q in range(2):
+    def pool_two(q):
         total = jnp.zeros((256, 128), F32)
         for half in range(2):
             p = ((3, 0), (1, 2))[q][half]
@@ -301,9 +290,9 @@
                 ),
             )
             for x in range(2):
-                v = leaky(acc[:, x * 128 : x * 128 + 128] + bias2[...])
-                out2[:, 2 * p + x] = v.reshape(32, 8, 128).astype(BF)
-                total = total + mm(v.astype(BF), table("pool_two", 128, 128, half * 256 + x * 128))
+                v = leaky(acc[:, x * 128 : x * 128 + 128] + bias2[...]).astype(BF)
+                l2[2 * p + x] = v
+                total = total + mm(v, table("pool_two", 128, 128, half * 256 + x * 128))
         pooled[...] = total
         mean = (pooled[pl.ds(0, 128, stride=2), :] + pooled[pl.ds(1, 128, stride=2), :]).astype(BF)
         own3[q + 1] = mean
@@ -317,6 +306,28 @@
                 send3(own3.at[1], own3.at[slot], x, gy)
         send3(hs3.at[1, q], hr3.at[0, q + 1], gx, yp)
         send3(hs3.at[0, q], hr3.at[1, q + 1], gx, ym)
+
+    for copy in second[4:]:
+        copy.wait()
+    for x in range(1, 9):
+        edge_rows(x)
+    pool_two(1)
+    for copy in second[:4]:
+        copy.wait()
+    for x in (0, 9):
+        edge_rows(x)
+    for copy in first:
+        copy.wait()
+    for x in (0, 9):
+        place(x)
+        shift(x)
+    a2[0, :, 0:128] += mm(t2[0, :, 0:768], fm[0:768, 0:128])
+    a2[3, :, 128:256] += mm(t2[2, :, 0:768], fm[0:768, 1152:1280])
+    pool_two(0)
+    for dx, dy in around:
+        greet(wide_sem.at[0], 2 * dx, 2 * dy)
+    for x in range(8):
+        out2[:, x] = l2[x].astype(F32).reshape(32, 8, 128).astype(BF)
 
     for dx in range(3):
         for dz in range(3):
@@ -505,6 +516,7 @@
             pltpu.VMEM((256, 128), F32),
             pltpu.VMEM((256, 128), F32),
             pltpu.VMEM((256, 128), F32),
+            pltpu.VMEM((8, 256, 128), BF),
             pltpu.VMEM((4, 128, 128), BF),
             pltpu.VMEM((2, 2, 32, 128), BF),
             pltpu.VMEM((2, 4, 32, 128), BF),

time: 30.9 us -> 32.4 us (1.049)
  Pallas kernels: 30.2 us -> 31.6 us
    pallas_call x1, Pallas kernels: 28.2 us -> 29.6 us  [shards(): pl.pallas_call(kernel, out_shape=(jax.ShapeDtypeStruct((32, 8, 8, 128), B...]
where the time goes in v9:
time: 32.4 us; the launch traced here: 32.3 us
  Pallas kernels  31.6 us (98%)
  between operations  0.64 us (2%)
    pallas_call x1, Pallas kernels, shards(): pl.pallas_call(kernel, out_shape=(jax.ShapeDtypeStruct((32, 8, 8, 128), B...  29.6 us
    pallas_call x1, Pallas kernels, shards(): pl.pallas_call(last, out_shape=(jax.ShapeDtypeStruct((32, 8, 8, 128), BF)...  1.97 us

profile of v9, /device:TPU:1, one launch (start us, length us, event | category | flops | bytes accessed | tf_op | source)
XLA Modules:
  0.0 32.3 jit_solution(7201897834707018866)
XLA Ops:
  0.6 29.6 %shard_map.103 = (bf16[32,8,8,128]{3,2,1,0:T(8,128)(2,1)S(1)}, bf16[64,4,4,64]{3,2,1,0:T(4,128)(2,1)S(1)}, bf16[128,8,128]{2,1,0:T(8,128)(2,1)S(1)}, bf16[9,4,64...) custom-call(bf16[32,8,8,128]{3,2,1,0:T(8,128)(2,1)} %feat.1, ...), custom_call_target="tpu_custom_call" | custom-call | tf_op jit(solution)/shard_map/pallas_call | solution.py:487
  30.3 2.0 %shard_map.104 = (bf16[32,8,8,128]{3,2,1,0:T(8,128)(2,1)}, bf16[64,4,4,64]{3,2,1,0:T(4,128)(2,1)}, bf16[512,2,128]{2,1,0:T(2,128)(2,1)}) custom-call(bf16[32,8,8,128]{3,2,1,0:T(8,128)(2,1)S(1)} %get-tuple-element.12.out2_in, bf16[64,4,4,64]{3,2,1,0:T(4,128)(2,1)S(1)} %get-tuple-element.13.out3_in, bf16[128,8,128]{2,1,0:T(8,128)(2,1)S(1)} %get-tuple-element.14.rb, ...), custom_call_target="tpu_custom_call" | custom-call | tf_op jit(solution)/shard_map/pallas_call | solution.py:539

commit v10 on v9

--- a/solution.py
+++ b/solution.py
@@ -311,7 +311,6 @@
         copy.wait()
     for x in range(1, 9):
         edge_rows(x)
-    pool_two(1)
     for copy in second[:4]:
         copy.wait()
     for x in (0, 9):
@@ -326,6 +325,7 @@
     pool_two(0)
     for dx, dy in around:
         greet(wide_sem.at[0], 2 * dx, 2 * dy)
+    pool_two(1)
     for x in range(8):
         out2[:, x] = l2[x].astype(F32).reshape(32, 8, 128).astype(BF)
 

time: 32.4 us -> 31.6 us (0.975)
  Pallas kernels: 31.6 us -> 30.8 us
    pallas_call x1, Pallas kernels: 29.6 us -> 28.9 us  [shards(): pl.pallas_call(kernel, out_shape=(jax.ShapeDtypeStruct((32, 8, 8, 128), B...]
where the time goes in v10:
time: 31.6 us; the launch traced here: 31.5 us
  Pallas kernels  30.8 us (97%)
  between operations  0.64 us (2%)
    pallas_call x1, Pallas kernels, shards(): pl.pallas_call(kernel, out_shape=(jax.ShapeDtypeStruct((32, 8, 8, 128), B...  28.9 us
    pallas_call x1, Pallas kernels, shards(): pl.pallas_call(last, out_shape=(jax.ShapeDtypeStruct((32, 8, 8, 128), BF)...  1.97 us

profile of v10, /device:TPU:1, one launch (start us, length us, event | category | flops | bytes accessed | tf_op | source)
XLA Modules:
  0.0 31.5 jit_solution(783445780070751887)
XLA Ops:
  0.6 28.9 %shard_map.103 = (bf16[32,8,8,128]{3,2,1,0:T(8,128)(2,1)S(1)}, bf16[64,4,4,64]{3,2,1,0:T(4,128)(2,1)S(1)}, bf16[128,8,128]{2,1,0:T(8,128)(2,1)S(1)}, bf16[9,4,64...) custom-call(bf16[32,8,8,128]{3,2,1,0:T(8,128)(2,1)} %feat.1, ...), custom_call_target="tpu_custom_call" | custom-call | tf_op jit(solution)/shard_map/pallas_call | solution.py:487
  29.5 2.0 %shard_map.104 = (bf16[32,8,8,128]{3,2,1,0:T(8,128)(2,1)}, bf16[64,4,4,64]{3,2,1,0:T(4,128)(2,1)}, bf16[512,2,128]{2,1,0:T(2,128)(2,1)}) custom-call(bf16[32,8,8,128]{3,2,1,0:T(8,128)(2,1)S(1)} %get-tuple-element.12.out2_in, bf16[64,4,4,64]{3,2,1,0:T(4,128)(2,1)S(1)} %get-tuple-element.13.out3_in, bf16[128,8,128]{2,1,0:T(8,128)(2,1)S(1)} %get-tuple-element.14.rb, ...), custom_call_target="tpu_custom_call" | custom-call | tf_op jit(solution)/shard_map/pallas_call | solution.py:539

commit v11 on v10

--- a/solution.py
+++ b/solution.py
@@ -214,6 +214,8 @@
         cut(edges[:, (x - 1) * 128 : x * 128], x)
     for copy in second[4:]:
         copy.start()
+    for dx, dy in around:
+        greet(wide_sem.at[2], dx, dy)
 
     for x in range(1, 9):
         shift(x)
@@ -264,6 +266,9 @@
         return carry
 
     lax.fori_loop(0, 4, inner, 0)
+    pl.semaphore_wait(wide_sem.at[2], 8)
+    for dx, dy in around:
+        greet(wide_sem.at[0], 2 * dx, 2 * dy)
 
     def edge_rows(x):
         v = jnp.concatenate([hr[0, x], hr[1, x]], axis=0).astype(F32)
@@ -323,8 +328,6 @@
     a2[0, :, 0:128] += mm(t2[0, :, 0:768], fm[0:768, 0:128])
     a2[3, :, 128:256] += mm(t2[2, :, 0:768], fm[0:768, 1152:1280])
     pool_two(0)
-    for dx, dy in around:
-        greet(wide_sem.at[0], 2 * dx, 2 * dy)
     pool_two(1)
     for x in range(8):
         out2[:, x] = l2[x].astype(F32).reshape(32, 8, 128).astype(BF)
@@ -525,7 +528,7 @@
             pltpu.VMEM((256, 256), BF),
             pltpu.VMEM((16, 8, 128), BF),
             dma((8,)), dma((8,)), dma((8,)), dma((8,)), dma((10,)), dma((10,)),
-            dma, dma, pltpu.SemaphoreType.REGULAR((2,)),
+            dma, dma, pltpu.SemaphoreType.REGULAR((3,)),
         ],
         compiler_params=pltpu.CompilerParams(
             collective_id=0, has_side_effects=True, vmem_limit_bytes=40 * 1024 * 1024

time: 31.6 us -> 30.9 us (0.978)
  Pallas kernels: 30.8 us -> 30.2 us
    pallas_call x1, Pallas kernels: 28.9 us -> 28.2 us  [shards(): pl.pallas_call(kernel, out_shape=(jax.ShapeDtypeStruct((32, 8, 8, 128), B...]
where the time goes in v11:
time: 30.9 us; the launch traced here: 30.8 us
  Pallas kernels  30.2 us (98%)
  between operations  0.64 us (2%)
    pallas_call x1, Pallas kernels, shards(): pl.pallas_call(kernel, out_shape=(jax.ShapeDtypeStruct((32, 8, 8, 128), B...  28.2 us
    pallas_call x1, Pallas kernels, shards(): pl.pallas_call(last, out_shape=(jax.ShapeDtypeStruct((32, 8, 8, 128), BF)...  1.97 us

profile of v11, /device:TPU:1, one launch (start us, length us, event | category | flops | bytes accessed | tf_op | source)
XLA Modules:
  0.0 30.8 jit_solution(123481076517892522)
XLA Ops:
  0.6 28.2 %shard_map.103 = (bf16[32,8,8,128]{3,2,1,0:T(8,128)(2,1)S(1)}, bf16[64,4,4,64]{3,2,1,0:T(4,128)(2,1)S(1)}, bf16[128,8,128]{2,1,0:T(8,128)(2,1)S(1)}, bf16[9,4,64...) custom-call(bf16[32,8,8,128]{3,2,1,0:T(8,128)(2,1)} %feat.1, ...), custom_call_target="tpu_custom_call" | custom-call | tf_op jit(solution)/shard_map/pallas_call | solution.py:490
  28.9 2.0 %shard_map.104 = (bf16[32,8,8,128]{3,2,1,0:T(8,128)(2,1)}, bf16[64,4,4,64]{3,2,1,0:T(4,128)(2,1)}, bf16[512,2,128]{2,1,0:T(2,128)(2,1)}) custom-call(bf16[32,8,8,128]{3,2,1,0:T(8,128)(2,1)S(1)} %get-tuple-element.12.out2_in, bf16[64,4,4,64]{3,2,1,0:T(4,128)(2,1)S(1)} %get-tuple-element.13.out3_in, bf16[128,8,128]{2,1,0:T(8,128)(2,1)S(1)} %get-tuple-element.14.rb, ...), custom_call_target="tpu_custom_call" | custom-call | tf_op jit(solution)/shard_map/pallas_call | solution.py:542

commit v12 on v10

--- a/solution.py
+++ b/solution.py
@@ -317,14 +317,14 @@
         edge_rows(x)
     for copy in first:
         copy.wait()
+    for dx, dy in around:
+        greet(wide_sem.at[0], 2 * dx, 2 * dy)
     for x in (0, 9):
         place(x)
         shift(x)
     a2[0, :, 0:128] += mm(t2[0, :, 0:768], fm[0:768, 0:128])
     a2[3, :, 128:256] += mm(t2[2, :, 0:768], fm[0:768, 1152:1280])
     pool_two(0)
-    for dx, dy in around:
-        greet(wide_sem.at[0], 2 * dx, 2 * dy)
     pool_two(1)
     for x in range(8):
         out2[:, x] = l2[x].astype(F32).reshape(32, 8, 128).astype(BF)

time: 31.6 us -> 30.9 us (0.978)
  Pallas kernels: 30.8 us -> 30.1 us
    pallas_call x1, Pallas kernels: 28.9 us -> 28.1 us  [shards(): pl.pallas_call(kernel, out_shape=(jax.ShapeDtypeStruct((32, 8, 8, 128), B...]
where the time goes in v12:
time: 30.9 us; the launch traced here: 30.8 us
  Pallas kernels  30.1 us (97%)
  between operations  0.64 us (2%)
    pallas_call x1, Pallas kernels, shards(): pl.pallas_call(kernel, out_shape=(jax.ShapeDtypeStruct((32, 8, 8, 128), B...  28.1 us
    pallas_call x1, Pallas kernels, shards(): pl.pallas_call(last, out_shape=(jax.ShapeDtypeStruct((32, 8, 8, 128), BF)...  1.97 us

profile of v12, /device:TPU:1, one launch (start us, length us, event | category | flops | bytes accessed | tf_op | source)
XLA Modules:
  0.0 30.8 jit_solution(3671200361279173263)
XLA Ops:
  0.6 28.1 %shard_map.103 = (bf16[32,8,8,128]{3,2,1,0:T(8,128)(2,1)S(1)}, bf16[64,4,4,64]{3,2,1,0:T(4,128)(2,1)S(1)}, bf16[128,8,128]{2,1,0:T(8,128)(2,1)S(1)}, bf16[9,4,64...) custom-call(bf16[32,8,8,128]{3,2,1,0:T(8,128)(2,1)} %feat.1, ...), custom_call_target="tpu_custom_call" | custom-call | tf_op jit(solution)/shard_map/pallas_call | solution.py:487
  28.8 2.0 %shard_map.104 = (bf16[32,8,8,128]{3,2,1,0:T(8,128)(2,1)}, bf16[64,4,4,64]{3,2,1,0:T(4,128)(2,1)}, bf16[512,2,128]{2,1,0:T(2,128)(2,1)}) custom-call(bf16[32,8,8,128]{3,2,1,0:T(8,128)(2,1)S(1)} %get-tuple-element.12.out2_in, bf16[64,4,4,64]{3,2,1,0:T(4,128)(2,1)S(1)} %get-tuple-element.13.out3_in, bf16[128,8,128]{2,1,0:T(8,128)(2,1)S(1)} %get-tuple-element.14.rb, ...), custom_call_target="tpu_custom_call" | custom-call | tf_op jit(solution)/shard_map/pallas_call | solution.py:539
